TPU v7x, 32 devices: a whole 2x2x4 slice. The times are simulated.
32 devices in a mesh: dp: 8 (over z, y), tensor: 4 (over x, core).
Axes of the slice: x: 2, y: 2, z: 4, core: 2. Of those that a mesh axis runs over, the one named last changes fastest.
Arguments:
- tokens: bfloat16 [16384, 1024], P(('dp', 'tensor')), may hold values from -6 to 6
- w_in: bfloat16 [1024, 3, 1024], P(None, None, 'tensor'), may hold values from -0.1875 to 0.1875
- conv_kernel: bfloat16 [3, 1024], P(None, 'tensor'), may hold values from -3.5 to 3.5
- w_out: bfloat16 [1024, 1024], P('tensor'), may hold values from -0.1875 to 0.1875
- w_gate: bfloat16 [1024, 4608], P(None, 'tensor'), may hold values from -0.1875 to 0.1875
- w_up: bfloat16 [1024, 4608], P(None, 'tensor'), may hold values from -0.1875 to 0.1875
- w_down: bfloat16 [4608, 1024], P('tensor'), may hold values from -0.09375 to 0.09375
- gain_mix: float32 [1024], replicated, may hold values from 0.25 to 1.75
- gain_mlp: float32 [1024], replicated, may hold values from 0.25 to 1.75
- cotangent: bfloat16 [16384, 1024], P(('dp', 'tensor')), may hold values from -6 to 6
Outputs:
- result: float32 [16384, 1024], P(('dp', 'tensor'))
- grad_tokens: float32 [16384, 1024], P(('dp', 'tensor'))
- grad_w_in: float32 [1024, 3, 1024], P(None, None, 'tensor')
- grad_kernel: float32 [3, 1024], P(None, 'tensor')
- grad_w_out: float32 [1024, 1024], P('tensor')
- grad_w_gate: float32 [1024, 4608], P(None, 'tensor')
- grad_w_up: float32 [1024, 4608], P(None, 'tensor')
- grad_w_down: float32 [4608, 1024], P('tensor')
- grad_gain_mix: float32 [1024], replicated
- grad_gain_mlp: float32 [1024], replicated
All inputs are finite; a program needn't handle non-finite values.
Results may differ from a plain program's by a relative error of at most 0.011.
Values may be sent and summed in bfloat16 or wider, within the bound.
A program may use at most 192 MiB of HBM per device.

v0:
```python
import jax
import jax.numpy as jnp
from jax import lax
from jax.sharding import PartitionSpec as P

LEN = 1024


EPSILON = 1e-05


def rms_scale(values):
    scale = lax.rsqrt(jnp.mean(values * values, axis=-1, keepdims=True) + EPSILON)
    return (values * scale, scale)


def norm_back(grad_norm, unit, scale, gain):
    weighted = grad_norm * gain
    return scale * (weighted - unit * jnp.mean(weighted * unit, axis=-1, keepdims=True))


def shift_down(values, shift_by):
    return jnp.pad(values, ((0, 0), (shift_by, 0), (0, 0)))[:, : values.shape[1], :]


def shift_up(values, shift_by):
    return jnp.pad(values, ((0, 0), (0, shift_by), (0, 0)))[:, shift_by:, :]


def dot_first(left, right):
    return lax.dot_general(
        left, right, (((0,), (0,)), ((), ())), preferred_element_type=jnp.float32
    )


def dot_last(left, right):
    return lax.dot_general(
        left, right, (((1,), (1,)), ((), ())), preferred_element_type=jnp.float32
    )


def shards(tokens, w_in, conv_kernel, w_out, w_gate, w_up, w_down, gain_mix, gain_mlp, cotangent):
    model_width = tokens.shape[1]
    channels = conv_kernel.shape[1]
    in_flat = w_in.reshape(model_width, 3 * channels)
    taps = conv_kernel.astype(jnp.float32)
    inputs = tokens.astype(jnp.float32)
    unit_one, scale_one = rms_scale(inputs)
    normed_one = lax.all_gather(
        (unit_one * gain_mix).astype(jnp.bfloat16), "tensor", axis=0, tiled=True
    )
    projected = jnp.dot(normed_one, in_flat, preferred_element_type=jnp.float32)
    b_part = projected[:, :channels]
    c_part = projected[:, channels : 2 * channels]
    x_part = projected[:, 2 * channels :]
    seq_gated = (b_part * x_part).reshape(-1, LEN, channels)
    back_one = shift_down(seq_gated, 1)
    back_two = shift_down(seq_gated, 2)
    convolved = (taps[0] * back_two + taps[1] * back_one + taps[2] * seq_gated).reshape(
        -1, channels
    )
    mixed_low = (c_part * convolved).astype(jnp.bfloat16)
    resid = inputs + lax.psum_scatter(
        jnp.dot(mixed_low, w_out, preferred_element_type=jnp.float32),
        "tensor",
        scatter_dimension=0,
        tiled=True,
    )
    unit_two, scale_two = rms_scale(resid)
    normed_two = lax.all_gather(
        (unit_two * gain_mlp).astype(jnp.bfloat16), "tensor", axis=0, tiled=True
    )
    gate_pre = jnp.dot(normed_two, w_gate, preferred_element_type=jnp.float32)
    up_pre = jnp.dot(normed_two, w_up, preferred_element_type=jnp.float32)
    sig_gate = jax.nn.sigmoid(gate_pre)
    activated = gate_pre * sig_gate
    hidden_low = (activated * up_pre).astype(jnp.bfloat16)
    result = resid + lax.psum_scatter(
        jnp.dot(hidden_low, w_down, preferred_element_type=jnp.float32).astype(jnp.bfloat16),
        "tensor",
        scatter_dimension=0,
        tiled=True,
    ).astype(jnp.float32)
    grad_full = lax.all_gather(cotangent, "tensor", axis=0, tiled=True)
    grad_down = dot_first(hidden_low, grad_full)
    grad_hidden = dot_last(grad_full, w_down)
    grad_gate_low = (grad_hidden * up_pre * sig_gate * (1.0 + gate_pre * (1.0 - sig_gate))).astype(
        jnp.bfloat16
    )
    grad_up_low = (grad_hidden * activated).astype(jnp.bfloat16)
    grad_wgate = dot_first(normed_two, grad_gate_low)
    grad_wup = dot_first(normed_two, grad_up_low)
    back_rows = lax.psum_scatter(
        dot_last(grad_gate_low, w_gate) + dot_last(grad_up_low, w_up),
        "tensor",
        scatter_dimension=0,
        tiled=True,
    )
    grad_resid = cotangent.astype(jnp.float32) + norm_back(back_rows, unit_two, scale_two, gain_mlp)
    grad_gain_two = jnp.sum(back_rows * unit_two, axis=0)
    grad_mixed = lax.all_gather(grad_resid.astype(jnp.bfloat16), "tensor", axis=0, tiled=True)
    grad_wout = dot_first(mixed_low, grad_mixed)
    grad_conv_out = dot_last(grad_mixed, w_out)
    grad_c = grad_conv_out * convolved
    seq_grad = (grad_conv_out * c_part).reshape(-1, LEN, channels)
    grad_gated = (
        taps[0] * shift_up(seq_grad, 2) + taps[1] * shift_up(seq_grad, 1) + taps[2] * seq_grad
    ).reshape(-1, channels)
    grad_taps = jnp.stack(
        [
            jnp.sum(seq_grad * back_two, axis=(0, 1)),
            jnp.sum(seq_grad * back_one, axis=(0, 1)),
            jnp.sum(seq_grad * seq_gated, axis=(0, 1)),
        ]
    )
    grad_proj_low = jnp.concatenate(
        [grad_gated * x_part, grad_c, grad_gated * b_part], axis=1
    ).astype(jnp.bfloat16)
    grad_win = dot_first(normed_one, grad_proj_low).reshape(model_width, 3, channels)
    back_first = lax.psum_scatter(
        dot_last(grad_proj_low, in_flat), "tensor", scatter_dimension=0, tiled=True
    )
    grad_gain_one = jnp.sum(back_first * unit_one, axis=0)
    grad_tokens = grad_resid + norm_back(back_first, unit_one, scale_one, gain_mix)
    grad_win, grad_taps, grad_wout, grad_wgate, grad_wup, grad_down = lax.psum(
        (grad_win, grad_taps, grad_wout, grad_wgate, grad_wup, grad_down), "dp"
    )
    grad_gain_one, grad_gain_two = lax.psum((grad_gain_one, grad_gain_two), ("dp", "tensor"))
    return (
        result,
        grad_tokens,
        grad_win,
        grad_taps,
        grad_wout,
        grad_wgate,
        grad_wup,
        grad_down,
        grad_gain_one,
        grad_gain_two,
    )


def swap(values, axis, step):
    count = lax.axis_size(axis)
    return lax.ppermute(values, axis, [(i, i ^ step) for i in range(count)])


def part(values, index):
    size = values.shape[0] // 2
    return lax.dynamic_slice_in_dim(values, index * size, size, axis=0)


def in_order(bit, mine, other):
    return jnp.concatenate(
        [jnp.where(bit == 0, mine, other), jnp.where(bit == 0, other, mine)], axis=0
    )


class Sum:
    def __init__(self, *pieces):
        self.place = lax.axis_index("dp")
        self.pieces = list(pieces)
        self.sent = None
        self.stage = 0
        self.start()

    def bit(self, step):
        return (self.place // step) % 2

    def steps(self):
        return {0: (1, 2), 1: (2, 1), 2: (4,), 3: (4,), 4: (2, 1), 5: (1, 2)}[self.stage]

    def start(self):
        steps = self.steps()
        if self.stage == 2:
            self.pieces = [jnp.concatenate(self.pieces, axis=0)]
        out = self.pieces
        if self.stage < 3:
            out = [part(p, 1 - self.bit(step)) for p, step in zip(out, steps)]
        self.sent = [swap(p, "dp", step) for p, step in zip(out, steps)]

    def advance(self, after=None):
        steps = self.steps()
        arrived = self.sent
        if after is not None:
            arrived = tied(arrived, after)
        if self.stage < 3:
            self.pieces = [
                (
                    part(p, self.bit(step)).astype(jnp.float32) + got.astype(jnp.float32)
                ).astype(jnp.bfloat16)
                for p, got, step in zip(self.pieces, arrived, steps)
            ]
        else:
            self.pieces = [
                in_order(self.bit(step), p, got)
                for p, got, step in zip(self.pieces, arrived, steps)
            ]
        if self.stage == 2:
            self.cut = self.sizes[0]
        if self.stage == 3:
            whole = self.pieces[0]
            self.pieces = [whole[: self.cut], whole[self.cut :]]
        if self.stage == 1:
            self.sizes = [p.shape[0] for p in self.pieces]
        self.stage += 1
        if self.stage < 6:
            self.start()

    def finish(self):
        while self.stage < 6:
            self.advance()
        return [piece.astype(jnp.float32) for piece in self.pieces]


def small_sum(values, axis):
    step = 1
    while step < lax.axis_size(axis):
        values = values + swap(values, axis, step)
        step *= 2
    return values


def tied(values, after):
    return lax.optimization_barrier((values, after))[0]


def gather_pair(own, core):
    return in_order(core, own, swap(own, "tensor", 1)), swap(own, "tensor", 2)


def gather_far(across, core, after):
    across = tied(across, after)
    return in_order(core, across, swap(across, "tensor", 1))


def sum_far(far, core):
    arrived = swap(part(far, 1 - core), "tensor", 1)
    return (part(far, core).astype(jnp.float32) + arrived.astype(jnp.float32)).astype(jnp.bfloat16)


def reduce_far(far, core):
    return swap(sum_far(far, core), "tensor", 2)


def reduce_near(near, core, crossed):
    arrived = swap(part(near, 1 - core), "tensor", 1)
    return (
        part(near, core).astype(jnp.float32)
        + arrived.astype(jnp.float32)
        + crossed.astype(jnp.float32)
    )


def dot(left, right):
    return jnp.dot(left, right, preferred_element_type=jnp.float32)


def down(values, shift_by):
    return jnp.pad(values, ((shift_by, 0), (0, 0)))[: values.shape[0]]


def up(values, shift_by):
    return jnp.pad(values, ((0, shift_by), (0, 0)))[shift_by:]


def conv_forward(normed, in_flat, taps):
    channels = taps.shape[1]
    projected = dot(normed, in_flat)
    b_part = projected[:, :channels]
    c_part = projected[:, channels : 2 * channels]
    x_part = projected[:, 2 * channels :]
    gated = b_part * x_part
    convolved = taps[0] * down(gated, 2) + taps[1] * down(gated, 1) + taps[2] * gated
    mixed = (c_part * convolved).astype(jnp.bfloat16)
    return mixed, (b_part, c_part, x_part, gated, convolved)


def conv_backward(grad_mixed, kept, w_out, taps):
    b_part, c_part, x_part, gated, convolved = kept
    grad_conv_out = dot_last(grad_mixed, w_out)
    grad_c = grad_conv_out * convolved
    grad_conv = grad_conv_out * c_part
    grad_gated = taps[0] * up(grad_conv, 2) + taps[1] * up(grad_conv, 1) + taps[2] * grad_conv
    grad_taps = jnp.stack(
        [
            jnp.sum(grad_conv * down(gated, 2), axis=0),
            jnp.sum(grad_conv * down(gated, 1), axis=0),
            jnp.sum(grad_conv * gated, axis=0),
        ]
    )
    grad_projected = jnp.concatenate(
        [grad_gated * x_part, grad_c, grad_gated * b_part], axis=1
    ).astype(jnp.bfloat16)
    return grad_projected, grad_taps


def mlp_forward(normed, w_gate, w_up):
    gate_pre = dot(normed, w_gate)
    up_pre = dot(normed, w_up)
    sig_gate = jax.nn.sigmoid(gate_pre)
    hidden = (gate_pre * sig_gate * up_pre).astype(jnp.bfloat16)
    return hidden, (gate_pre, up_pre, sig_gate)


def mlp_backward(grad_out, kept, w_gate, w_up, w_down):
    gate_pre, up_pre, sig_gate = kept
    grad_hidden = dot_last(grad_out, w_down)
    grad_gate = (grad_hidden * up_pre * sig_gate * (1.0 + gate_pre * (1.0 - sig_gate))).astype(
        jnp.bfloat16
    )
    grad_up = (grad_hidden * gate_pre * sig_gate).astype(jnp.bfloat16)
    back = (dot_last(grad_gate, w_gate) + dot_last(grad_up, w_up)).astype(jnp.bfloat16)
    return grad_gate, grad_up, back


def pair_shards(
    tokens, w_in, conv_kernel, w_out, w_gate, w_up, w_down, gain_mix, gain_mlp, cotangent
):
    low = jnp.bfloat16
    model_width = tokens.shape[1]
    channels = conv_kernel.shape[1]
    core = lax.axis_index("tensor") % 2
    in_flat = w_in.reshape(model_width, 3 * channels)
    taps = conv_kernel.astype(jnp.float32)
    inputs = tokens.astype(jnp.float32)
    unit_one, scale_one = rms_scale(inputs)
    one_near, across = gather_pair((unit_one * gain_mix).astype(low), core)
    mixed_near, kept_near = conv_forward(one_near, in_flat, taps)
    branch_near = dot(mixed_near, w_out).astype(low)
    one_far = gather_far(across, core, branch_near)
    mixed_far, kept_far = conv_forward(one_far, in_flat, taps)
    branch_sum = sum_far(dot(mixed_far, w_out).astype(low), core)
    crossed = swap(branch_sum, "tensor", 2)
    resid = inputs + reduce_near(branch_near, core, crossed)
    unit_two, scale_two = rms_scale(resid)
    two_near, across = gather_pair((unit_two * gain_mlp).astype(low), core)
    cot_near = in_order(core, cotangent, swap(cotangent, "tensor", 1))
    cot_across = swap(tied(cotangent, across), "tensor", 2)
    hidden_near, mlp_near = mlp_forward(two_near, w_gate, w_up)
    gate_near, up_near, back_near = mlp_backward(cot_near, mlp_near, w_gate, w_up, w_down)
    two_far = gather_far(across, core, back_near)
    hidden_far, mlp_far = mlp_forward(two_far, w_gate, w_up)
    out_far = dot(hidden_far, w_down).astype(low)
    out_sum = sum_far(out_far, core)
    down_near = dot_first(hidden_near, cot_near)
    wgate_near = dot_first(two_near, gate_near)
    wup_near = dot_first(two_near, up_near)
    out_near = dot(hidden_near, w_down).astype(low)
    cot_far = gather_far(cot_across, core, (out_sum, down_near, wgate_near, wup_near, out_near))
    grad_down = (down_near + dot_first(hidden_far, cot_far)).astype(low)
    cut = grad_down.shape[0] // 2 // 128 * 128 + 256
    sum_down = Sum(grad_down[:cut], grad_down[cut:])
    gate_far, up_far, back_far = mlp_backward(
        tied(cot_far, grad_down), mlp_far, w_gate, w_up, w_down
    )
    back_sum = sum_far(back_far, core)
    back_crossed = swap(back_sum, "tensor", 2)
    sum_down.advance(after=back_sum)
    gate_far, up_far = tied((gate_far, up_far), back_sum)
    grad_gate = (wgate_near + dot_first(two_far, gate_far)).astype(low)
    grad_up = (wup_near + dot_first(two_far, up_far)).astype(low)
    sum_mlp = Sum(grad_gate, grad_up)
    sum_down.advance(after=grad_up)
    back_rows = reduce_near(tied(back_near, grad_gate), core, tied(back_crossed, grad_up))
    grad_resid = cotangent.astype(jnp.float32) + norm_back(back_rows, unit_two, scale_two, gain_mlp)
    gain_two = jnp.sum(back_rows * unit_two, axis=0)
    gm_near, across = gather_pair(grad_resid.astype(low), core)
    gp_near, taps_near = conv_backward(gm_near, kept_near, w_out, taps)
    first_near = dot_last(gp_near, in_flat).astype(low)
    sum_down.advance(after=first_near)
    sum_mlp.advance(after=first_near)
    gm_far = gather_far(across, core, first_near)
    gp_far, taps_far = conv_backward(gm_far, kept_far, w_out, taps)
    first_sum = sum_far(dot_last(gp_far, in_flat).astype(low), core)
    first_crossed = swap(first_sum, "tensor", 2)
    sum_down.advance(after=first_sum)
    gp_far = tied(gp_far, first_sum)
    grad_blocks = jnp.concatenate(
        [
            dot_first(one_near, gp_near[:, i * channels : (i + 1) * channels])
            + dot_first(one_far, gp_far[:, i * channels : (i + 1) * channels])
            for i in range(3)
        ],
        axis=0,
    ).astype(low)
    grad_wout = (dot_first(gm_near, mixed_near) + dot_first(gm_far, mixed_far)).astype(low)
    sum_conv = Sum(grad_blocks, grad_wout)
    sum_mlp.advance(after=grad_blocks)
    sum_down.advance(after=grad_blocks)
    back_first = reduce_near(tied(first_near, grad_wout), core, tied(first_crossed, sum_mlp.pieces))
    gain_one = jnp.sum(back_first * unit_one, axis=0)
    grad_tokens = grad_resid + norm_back(back_first, unit_one, scale_one, gain_mix)
    gains = small_sum(jnp.stack([gain_one, gain_two]), "tensor")
    out_crossed = swap(tied(out_sum, first_crossed), "tensor", 2)
    small = jnp.concatenate([gains.reshape(-1), (taps_near + taps_far).reshape(-1)])
    done = (sum_mlp.pieces, sum_down.pieces)
    step = 1
    for each in (
        sum_mlp, sum_conv, sum_down, None, sum_conv, sum_mlp, None, sum_conv, sum_mlp, None,
        sum_conv, sum_mlp, sum_conv, sum_conv,
    ):
        if each is sum_mlp and each.stage == 4:
            result = resid + reduce_near(tied(out_near, done), core, out_crossed)
            done = result
        if each is None:
            small = small + swap(tied(small, done), "dp", step)
            step *= 2
            done = small
        else:
            each.advance(after=done)
            done = each.pieces
    grad_down = jnp.concatenate(sum_down.finish(), axis=0)
    grad_wgate, grad_wup = sum_mlp.finish()
    grad_blocks, grad_wout = sum_conv.finish()
    grad_win = grad_blocks.reshape(3, model_width, channels).transpose(1, 0, 2)
    grad_wout = grad_wout.T
    return (
        result,
        grad_tokens,
        grad_win,
        small[2 * model_width :].reshape(3, channels),
        grad_wout,
        grad_wgate,
        grad_wup,
        grad_down,
        small[:model_width],
        small[model_width : 2 * model_width],
    )


def solution(mesh):
    placed = (
        P(("dp", "tensor"), None),
        P(None, None, "tensor"),
        P(None, "tensor"),
        P("tensor", None),
        P(None, "tensor"),
        P(None, "tensor"),
        P("tensor", None),
        P(),
        P(),
        P(("dp", "tensor"), None),
    )
    paired = mesh.shape["tensor"] == 4 and mesh.shape["dp"] == 8
    return jax.shard_map(
        pair_shards if paired else shards,
        mesh=mesh,
        in_specs=placed,
        out_specs=(
            P(("dp", "tensor"), None),
            P(("dp", "tensor"), None),
            P(None, None, "tensor"),
            P(None, "tensor"),
            P("tensor", None),
            P(None, "tensor"),
            P(None, "tensor"),
            P("tensor", None),
            P(),
            P(),
        ),
        check_vma=False,
    )
```

profile of v0, /device:TPU:0, one launch (start us, length us, event | category | flops | bytes accessed | tf_op | source)
XLA Modules:
  0.0 459.5 jit_solution(8705703207879367696)
XLA Ops:
  2.3 2.5 fusion.4
  5.3 2.6 collective-permute-start.2
  7.9 2.6 copy.21
  18.4 13.5 %collective-permute-done.2 = bf16[512,1024]{1,0:T(8,128)(2,1)} collective-permute-done((bf16[512,1024]{1,0:T(8,128)(2,1)}, bf16[512,1024]{1,0:T(8,128)(2,1)}, u32[]{:S(2)}, u32[]{:S(2)}) %collective-permute-start.2) | collective-permute-done | bytes 1048608 | tf_op jit(solution)/shard_map/ppermute | solution.py:145
  31.9 3.0 collective-permute-done.3
  50.1 23.4 %collective-permute-done.5 = bf16[512,1024]{1,0:T(8,128)(2,1)S(1)} collective-permute-done((bf16[512,1024]{1,0:T(8,128)(2,1)S(1)}, bf16[512,1024]{1,0:T(8,128)(2,1)S(1)}, u32[]{:S(2)}, u32[]{:S(2)}) %collective-permute-start.5) | collective-permute-done | bytes 1048608 | tf_op jit(solution)/shard_map/ppermute | solution.py:145
  76.6 2.9 fusion.20
  81.8 3.1 fusion.58
  85.0 6.7 %multiply_convert_fusion.5 = (bf16[1024,1152]{1,0:T(8,128)(2,1)}, bf16[1024,1152]{1,0:T(8,128)(2,1)S(1)}, bf16[1024,1152]{1,0:T(8,128)(2,1)}) fusion(f32[1024,1152]{1,0:T(8,128)S(1)} %fusion.58, f32[1024,1152]{1,0:T(8,128)S(1)} %fusion.20, bf16[1024,1152]{1,0:T(8,128)(2,1)S(1)} %copy-done, bf16[512,1024]{1,0:T(8,128)(2,1)S(1)} %get-tuple-element.168, ...), kind=kOutput, calls=%fused_computation.9 | convolution fusion | flops 2438987776 | bytes 20971520 | tf_op jit(solution)/shard_map/dot_general | solution.py:256
  91.8 2.9 fusion.68
  94.7 4.1 add_convert_fusion.4
  98.8 5.2 %collective-permute-done.8 = bf16[512,1024]{1,0:T(8,128)(2,1)S(1)} collective-permute-done((bf16[512,1024]{1,0:T(8,128)(2,1)S(1)}, bf16[512,1024]{1,0:T(8,128)(2,1)S(1)}, u32[]{:S(2)}, u32[]{:S(2)}) %collective-permute-start.8) | collective-permute-done | bytes 1048608 | tf_op jit(solution)/shard_map/ppermute | solution.py:145
  105.7 4.6 %fusion.55 = f32[1024,1152]{1,0:T(8,128)} fusion(bf16[1024,1152]{1,0:T(8,128)(2,1)S(1)} %copy-done.94, bf16[512,1024]{1,0:T(8,128)(2,1)S(1)} %get-tuple-element.168, bf16[512,1024]{1,0:T(8,128)(2,1)S(1)} %get-tuple-element.167), kind=kOutput, calls=%fused_computation.249 | convolution fusion | flops 2420113408 | bytes 9175040 | tf_op jit(solution)/shard_map/dot_general | solution.py:31
  110.3 4.6 fusion.56
  115.0 2.9 fusion.54
  117.9 17.5 %multiply_convert_fusion.2 = (bf16[1024,1152]{1,0:T(8,128)(2,1)S(1)}, f32[1024,1152]{1,0:T(8,128)}) fusion(f32[1024,1152]{1,0:T(8,128)S(1)} %fusion.54, bf16[1024,1152]{1,0:T(8,128)(2,1)S(1)} %copy-done, bf16[512,1024]{1,0:T(8,128)(2,1)S(1)} %get-tuple-element.164, bf16[512,1024]{1,0:T(8,128)(2,1)S(1)} %get-tuple-element.163), kind=kOutput, calls=%fused_computation.5 | convolution fusion | flops 2427191296 | bytes 16252928 | tf_op jit(solution)/shard_map/dot_general | solution.py:256
  135.4 3.1 convolution_convert_fusion
  138.9 2.7 fusion.19
  141.6 4.1 convolution_convert_fusion.1
  149.8 4.0 add_convert_fusion.2
  154.0 5.9 %multiply_convert_fusion = (bf16[1024,1152]{1,0:T(8,128)(2,1)S(1)}, bf16[1024,1152]{1,0:T(8,128)(2,1)S(1)}) fusion(f32[1024,1152]{1,0:T(8,128)S(1)} %fusion.54, f32[1024,1152]{1,0:T(8,128)} %get-tuple-element.207, bf16[1024,1024]{1,0:T(8,128)(2,1)S(1)} %pad_maximum_fusion.7, bf16[1152,1024]{1,0:T(8,128)(2,1)S(1)} %copy-done.87), kind=kOutput, calls=%fused_computation.2 | convolution fusion | flops 2431254528 | bytes 18612224 | tf_op jit(solution)/shard_map/dot_general | solution.py:37
  159.9 2.9 fusion.69
  162.8 3.1 add_convert_fusion.3
  178.9 7.0 %collective-permute-done.28 = bf16[192,1024]{1,0:T(8,128)(2,1)} collective-permute-done((bf16[192,1024]{1,0:T(8,128)(2,1)}, bf16[192,1024]{1,0:T(8,128)(2,1)}, u32[]{:S(2)}, u32[]{:S(2)}) %collective-permute-start.28) | collective-permute-done | bytes 393248 | tf_op jit(solution)/shard_map/ppermute | solution.py:145
  185.9 5.2 %collective-permute-done.27 = bf16[384,1024]{1,0:T(8,128)(2,1)} collective-permute-done((bf16[384,1024]{1,0:T(8,128)(2,1)}, bf16[384,1024]{1,0:T(8,128)(2,1)}, u32[]{:S(2)}, u32[]{:S(2)}) %collective-permute-start.27) | collective-permute-done | bytes 786464 | tf_op jit(solution)/shard_map/ppermute | solution.py:145
  193.9 4.9 %add_convert_fusion.1 = bf16[1024,1152]{1,0:T(8,128)(2,1)S(1)} fusion(f32[1024,1152]{1,0:T(8,128)} %fusion.56, bf16[1024,1152]{1,0:T(8,128)(2,1)S(1)} %copy-done.92, bf16[512,1024]{1,0:T(8,128)(2,1)S(1)} %copy-done.66, bf16[512,1024]{1,0:T(8,128)(2,1)S(1)} %get-tuple-element.163), kind=kOutput, calls=%fused_computation.1 | convolution fusion | flops 2422472704 | bytes 11534336 | tf_op jit(solution)/shard_map/dot_general | solution.py:31
  202.2 3.7 add_convert_fusion
  212.5 2.6 collective-permute-start.31
  219.1 3.1 convolution_convert_fusion.5
  222.2 20.5 %collective-permute-done.31 = bf16[144,1024]{1,0:T(8,128)(2,1)S(1)} collective-permute-done((bf16[144,1024]{1,0:T(8,128)(2,1)S(1)}, bf16[144,1024]{1,0:T(8,128)(2,1)S(1)}, u32[]{:S(2)}, u32[]{:S(2)}) %collective-permute-start.31) | collective-permute-done | bytes 294944 | tf_op jit(solution)/shard_map/ppermute | solution.py:145
  243.7 3.4 collective-permute-start.32
  279.5 2.8 collective-permute-done.34
  284.4 4.4 collective-permute-done.33
  292.3 17.7 %collective-permute-done.26 = bf16[256,1152]{1,0:T(8,128)(2,1)S(1)} collective-permute-done((bf16[256,1152]{1,0:T(8,128)(2,1)S(1)}, bf16[256,1152]{1,0:T(8,128)(2,1)S(1)}, u32[]{:S(2)}, u32[]{:S(2)}) %collective-permute-start.26) | collective-permute-done | bytes 589856 | tf_op jit(solution)/shard_map/ppermute | solution.py:145
  319.1 3.6 collective-permute-start.35
  323.4 3.1 collective-permute-done.41
  326.5 12.0 %collective-permute-done.43 = bf16[256,1152]{1,0:T(8,128)(2,1)} collective-permute-done((bf16[256,1152]{1,0:T(8,128)(2,1)}, bf16[256,1152]{1,0:T(8,128)(2,1)}, u32[]{:S(2)}, u32[]{:S(2)}) %collective-permute-start.43) | collective-permute-done | bytes 589856 | tf_op jit(solution)/shard_map/ppermute | solution.py:145
  338.5 4.6 %collective-permute-done.35 = bf16[768,256]{1,0:T(8,128)(2,1)} collective-permute-done((bf16[768,256]{1,0:T(8,128)(2,1)}, bf16[768,256]{1,0:T(8,128)(2,1)}, u32[]{:S(2)}, u32[]{:S(2)}) %collective-permute-start.35) | collective-permute-done | bytes 393248 | tf_op jit(solution)/shard_map/ppermute | solution.py:145
  354.9 6.5 %collective-permute-done.42 = bf16[512,256]{1,0:T(8,128)(2,1)} collective-permute-done((bf16[512,256]{1,0:T(8,128)(2,1)}, bf16[512,256]{1,0:T(8,128)(2,1)}, u32[]{:S(2)}, u32[]{:S(2)}) %collective-permute-start.42) | collective-permute-done | bytes 262176 | tf_op jit(solution)/shard_map/ppermute | solution.py:145
  364.2 4.0 fusion.9
  370.3 6.0 %collective-permute-done.58 = bf16[192,1024]{1,0:T(8,128)(2,1)S(1)} collective-permute-done((bf16[192,1024]{1,0:T(8,128)(2,1)}, bf16[192,1024]{1,0:T(8,128)(2,1)S(1)}, u32[]{:S(2)}, u32[]{:S(2)}) %collective-permute-start.58) | collective-permute-done | bytes 393248 | tf_op jit(solution)/shard_map/ppermute | solution.py:145
  379.6 14.5 %collective-permute-done.48 = bf16[256,1152]{1,0:T(8,128)(2,1)S(1)} collective-permute-done((bf16[256,1152]{1,0:T(8,128)(2,1)S(1)}, bf16[256,1152]{1,0:T(8,128)(2,1)S(1)}, u32[]{:S(2)}, u32[]{:S(2)}) %collective-permute-start.48) | collective-permute-done | bytes 589856 | tf_op jit(solution)/shard_map/ppermute | solution.py:145
  401.5 2.8 maximum_convert_fusion
  406.1 22.9 %collective-permute-done.52 = bf16[256,256]{1,0:T(8,128)(2,1)S(1)} collective-permute-done((bf16[256,256]{1,0:T(8,128)(2,1)S(1)}, bf16[256,256]{1,0:T(8,128)(2,1)S(1)}, u32[]{:S(2)}, u32[]{:S(2)}) %collective-permute-start.52) | collective-permute-done | bytes 131104 | tf_op jit(solution)/shard_map/ppermute | solution.py:145
  429.0 4.5 collective-permute-done.51
  440.3 2.5 fusion.61
  442.8 2.5 fusion.62
  445.2 8.7 %collective-permute-done.55 = bf16[1536,256]{1,0:T(8,128)(2,1)S(1)} collective-permute-done((bf16[1536,256]{1,0:T(8,128)(2,1)S(1)}, bf16[1536,256]{1,0:T(8,128)(2,1)S(1)}, u32[]{:S(2)}, u32[]{:S(2)}) %collective-permute-start.55) | collective-permute-done | bytes 786464 | tf_op jit(solution)/shard_map/ppermute | solution.py:145
  (425 shorter events, 155.6 us)
Async XLA Ops:
  5.3 26.6 %collective-permute-start.2 = (bf16[512,1024]{1,0:T(8,128)(2,1)}, bf16[512,1024]{1,0:T(8,128)(2,1)}, u32[]{:S(2)}, u32[]{:S(2)}) collective-permute-start(bf16[512,1024]{1,0:T(8,128)(2,1)} %fusion.4), channel_id=1, source_target_pairs={{0,2},{1,3},{2,0},{3,1},{4,6},{5,7},{6,4},{7,5},{8,10},{9,11},{10,... | collective-permute-start | bytes 3145736 | tf_op jit(solution)/shard_map/ppermute | solution.py:145
  48.2 25.3 %collective-permute-start.5 = (bf16[512,1024]{1,0:T(8,128)(2,1)S(1)}, bf16[512,1024]{1,0:T(8,128)(2,1)S(1)}, u32[]{:S(2)}, u32[]{:S(2)}) collective-permute-start(bf16[512,1024]{1,0:T(8,128)(2,1)S(1)} %add_convert_fusion.10), channel_id=1, source_target_pairs={{0,2},{1,3},{2,0},{3,1},{4,6},{5,7},{6,4},{7,5},{8,10},{9,11},{10,... | collective-permute-start | bytes 3145736 | tf_op jit(solution)/shard_map/ppermute | solution.py:145
  50.0 24.5 %collective-permute-start.7 = (bf16[512,1024]{1,0:T(8,128)(2,1)S(1)}, bf16[512,1024]{1,0:T(8,128)(2,1)S(1)}, u32[]{:S(2)}, u32[]{:S(2)}) collective-permute-start(bf16[512,1024]{1,0:T(8,128)(2,1)S(1)} %copy-done.25), channel_id=1, source_target_pairs={{0,1},{1,0},{2,3},{3,2},{4,5},{5,4},{6,7},{7,6},{8,9},{9,8},{10,11... | collective-permute-start | bytes 3145736 | tf_op jit(solution)/shard_map/ppermute | solution.py:145
  74.5 6.9 %collective-permute-start.6 = (bf16[512,1024]{1,0:T(8,128)(2,1)S(1)}, bf16[512,1024]{1,0:T(8,128)(2,1)S(1)}, u32[]{:S(2)}, u32[]{:S(2)}) collective-permute-start(bf16[512,1024]{1,0:T(8,128)(2,1)S(1)} %multiply_convert_fusion.6), channel_id=1, source_target_pairs={{0,1},{1,0},{2,3},{3,2},{4,5},{5,4},{6,7},{7,6},{8,9},{9,8},{10,11... | collective-permute-start | bytes 3145736 | tf_op jit(solution)/shard_map/ppermute | solution.py:145
  79.5 24.4 %collective-permute-start.8 = (bf16[512,1024]{1,0:T(8,128)(2,1)S(1)}, bf16[512,1024]{1,0:T(8,128)(2,1)S(1)}, u32[]{:S(2)}, u32[]{:S(2)}) collective-permute-start(bf16[512,1024]{1,0:T(8,128)(2,1)S(1)} %multiply_convert_fusion.6), channel_id=1, source_target_pairs={{0,2},{1,3},{2,0},{3,1},{4,6},{5,7},{6,4},{7,5},{8,10},{9,11},{10,... | collective-permute-start | bytes 3145736 | tf_op jit(solution)/shard_map/ppermute | solution.py:145
  104.0 10.9 %collective-permute-start.9 = (bf16[512,1024]{1,0:T(8,128)(2,1)S(1)}, bf16[512,1024]{1,0:T(8,128)(2,1)S(1)}, u32[]{:S(2)}, u32[]{:S(2)}) collective-permute-start(bf16[512,1024]{1,0:T(8,128)(2,1)S(1)} %collective-permute-done.8), channel_id=1, source_target_pairs={{0,1},{1,0},{2,3},{3,2},{4,5},{5,4},{6,7},{7,6},{8,9},{9,8},{10,11... | collective-permute-start | bytes 3145736 | tf_op jit(solution)/shard_map/ppermute | solution.py:145
  104.0 43.0 %collective-permute-start.10 = (bf16[512,1024]{1,0:T(8,128)(2,1)S(1)}, bf16[512,1024]{1,0:T(8,128)(2,1)S(1)}, u32[]{:S(2)}, u32[]{:S(2)}) collective-permute-start(bf16[512,1024]{1,0:T(8,128)(2,1)S(1)} %copy-done.25), channel_id=1, source_target_pairs={{0,2},{1,3},{2,0},{3,1},{4,6},{5,7},{6,4},{7,5},{8,10},{9,11},{10,... | collective-permute-start | bytes 3145736 | tf_op jit(solution)/shard_map/ppermute | solution.py:145
  138.6 7.0 %collective-permute-start.11 = (bf16[512,1024]{1,0:T(8,128)(2,1)S(1)}, bf16[512,1024]{1,0:T(8,128)(2,1)S(1)}, u32[]{:S(2)}, u32[]{:S(2)}) collective-permute-start(bf16[512,1024]{1,0:T(8,128)(2,1)S(1)} %constant_dynamic-slice_fusion.17), channel_id=1, source_target_pairs={{0,1},{1,0},{2,3},{3,2},{4,5},{5,4},{6,7},{7,6},{8,9},{9,8},{10,11... | collective-permute-start | bytes 3145736 | tf_op jit(solution)/shard_map/ppermute | solution.py:145
  168.3 7.9 %collective-permute-start.13 = (bf16[512,1024]{1,0:T(8,128)(2,1)}, bf16[512,1024]{1,0:T(8,128)(2,1)}, u32[]{:S(2)}, u32[]{:S(2)}) collective-permute-start(bf16[512,1024]{1,0:T(8,128)(2,1)} %constant_dynamic-slice_fusion.16), channel_id=1, source_target_pairs={{0,1},{1,0},{2,3},{3,2},{4,5},{5,4},{6,7},{7,6},{8,9},{9,8},{10,11... | collective-permute-start | bytes 3145736 | tf_op jit(solution)/shard_map/ppermute | solution.py:145
  171.1 20.0 %collective-permute-start.27 = (bf16[384,1024]{1,0:T(8,128)(2,1)}, bf16[384,1024]{1,0:T(8,128)(2,1)}, u32[]{:S(2)}, u32[]{:S(2)}) collective-permute-start(bf16[384,1024]{1,0:T(8,128)(2,1)} %constant_dynamic-slice_fusion.7), channel_id=1, source_target_pairs={{0,4},{4,0},{8,12},{12,8},{16,20},{20,16},{24,28},{28,24},{1,5},{5... | collective-permute-start | bytes 2359304 | tf_op jit(solution)/shard_map/ppermute | solution.py:145
  174.6 11.3 %collective-permute-start.28 = (bf16[192,1024]{1,0:T(8,128)(2,1)}, bf16[192,1024]{1,0:T(8,128)(2,1)}, u32[]{:S(2)}, u32[]{:S(2)}) collective-permute-start(bf16[192,1024]{1,0:T(8,128)(2,1)} %constant_dynamic-slice_fusion.6), channel_id=1, source_target_pairs={{0,8},{4,12},{8,0},{12,4},{16,24},{20,28},{24,16},{28,20},{1,9},{5... | collective-permute-start | bytes 1179656 | tf_op jit(solution)/shard_map/ppermute | solution.py:145
  178.3 27.6 %collective-permute-start.15 = (bf16[512,1024]{1,0:T(8,128)(2,1)S(1)}, bf16[512,1024]{1,0:T(8,128)(2,1)S(1)}, u32[]{:S(2)}, u32[]{:S(2)}) collective-permute-start(bf16[512,1024]{1,0:T(8,128)(2,1)S(1)} %add_convert_fusion.8), channel_id=1, source_target_pairs={{0,2},{1,3},{2,0},{3,1},{4,6},{5,7},{6,4},{7,5},{8,10},{9,11},{10,... | collective-permute-start | bytes 3145736 | tf_op jit(solution)/shard_map/ppermute | solution.py:145
  192.3 18.5 %collective-permute-start.30 = (bf16[96,1024]{1,0:T(8,128)(2,1)S(1)}, bf16[96,1024]{1,0:T(8,128)(2,1)S(1)}, u32[]{:S(2)}, u32[]{:S(2)}) collective-permute-start(bf16[96,1024]{1,0:T(8,128)(2,1)S(1)} %constant_dynamic-slice_fusion.4), channel_id=1, source_target_pairs={{0,4},{4,0},{8,12},{12,8},{16,20},{20,16},{24,28},{28,24},{1,5},{5... | collective-permute-start | bytes 589832 | tf_op jit(solution)/shard_map/ppermute | solution.py:145
  198.9 7.1 %collective-permute-start.14 = (bf16[512,1024]{1,0:T(8,128)(2,1)S(1)}, bf16[512,1024]{1,0:T(8,128)(2,1)S(1)}, u32[]{:S(2)}, u32[]{:S(2)}) collective-permute-start(bf16[512,1024]{1,0:T(8,128)(2,1)S(1)} %constant_dynamic-slice_fusion.15), channel_id=1, source_target_pairs={{0,1},{1,0},{2,3},{3,2},{4,5},{5,4},{6,7},{7,6},{8,9},{9,8},{10,11... | collective-permute-start | bytes 3145736 | tf_op jit(solution)/shard_map/ppermute | solution.py:145
  200.6 11.4 %collective-permute-start.29 = (bf16[192,1024]{1,0:T(8,128)(2,1)S(1)}, bf16[192,1024]{1,0:T(8,128)(2,1)S(1)}, u32[]{:S(2)}, u32[]{:S(2)}) collective-permute-start(bf16[192,1024]{1,0:T(8,128)(2,1)S(1)} %constant_dynamic-slice_fusion.5), channel_id=1, source_target_pairs={{0,8},{4,12},{8,0},{12,4},{16,24},{20,28},{24,16},{28,20},{1,9},{5... | collective-permute-start | bytes 1179656 | tf_op jit(solution)/shard_map/ppermute | solution.py:145
  209.4 6.2 %collective-permute-start.16 = (bf16[512,1024]{1,0:T(8,128)(2,1)S(1)}, bf16[512,1024]{1,0:T(8,128)(2,1)S(1)}, u32[]{:S(2)}, u32[]{:S(2)}) collective-permute-start(bf16[512,1024]{1,0:T(8,128)(2,1)S(1)} %get-tuple-element.140), channel_id=1, source_target_pairs={{0,1},{1,0},{2,3},{3,2},{4,5},{5,4},{6,7},{7,6},{8,9},{9,8},{10,11... | collective-permute-start | bytes 3145736 | tf_op jit(solution)/shard_map/ppermute | solution.py:145
  209.6 37.5 %collective-permute-start.23 = (bf16[512,1152]{1,0:T(8,128)(2,1)S(1)}, bf16[512,1152]{1,0:T(8,128)(2,1)S(1)}, u32[]{:S(2)}, u32[]{:S(2)}) collective-permute-start(bf16[512,1152]{1,0:T(8,128)(2,1)S(1)} %constant_dynamic-slice_fusion.10), channel_id=1, source_target_pairs={{0,8},{4,12},{8,0},{12,4},{16,24},{20,28},{24,16},{28,20},{1,9},{5... | collective-permute-start | bytes 3538952 | tf_op jit(solution)/shard_map/ppermute | solution.py:145
  210.2 36.9 %collective-permute-start.22 = (bf16[512,1152]{1,0:T(8,128)(2,1)S(1)}, bf16[512,1152]{1,0:T(8,128)(2,1)S(1)}, u32[]{:S(2)}, u32[]{:S(2)}) collective-permute-start(bf16[512,1152]{1,0:T(8,128)(2,1)S(1)} %constant_dynamic-slice_fusion.11), channel_id=1, source_target_pairs={{0,4},{4,0},{8,12},{12,8},{16,20},{20,16},{24,28},{28,24},{1,5},{5... | collective-permute-start | bytes 3538952 | tf_op jit(solution)/shard_map/ppermute | solution.py:145
  212.5 30.3 %collective-permute-start.31 = (bf16[144,1024]{1,0:T(8,128)(2,1)S(1)}, bf16[144,1024]{1,0:T(8,128)(2,1)S(1)}, u32[]{:S(2)}, u32[]{:S(2)}) collective-permute-start(bf16[144,1024]{1,0:T(8,128)(2,1)S(1)} %fusion.41), channel_id=1, source_target_pairs={{0,16},{4,20},{8,24},{12,28},{16,0},{20,4},{24,8},{28,12},{1,17},{... | collective-permute-start | bytes 884744 | tf_op jit(solution)/shard_map/ppermute | solution.py:145
  215.1 32.0 %collective-permute-start.17 = (bf16[512,1024]{1,0:T(8,128)(2,1)S(1)}, bf16[512,1024]{1,0:T(8,128)(2,1)S(1)}, u32[]{:S(2)}, u32[]{:S(2)}) collective-permute-start(bf16[512,1024]{1,0:T(8,128)(2,1)S(1)} %get-tuple-element.140), channel_id=1, source_target_pairs={{0,2},{1,3},{2,0},{3,1},{4,6},{5,7},{6,4},{7,5},{8,10},{9,11},{10,... | collective-permute-start | bytes 3145736 | tf_op jit(solution)/shard_map/ppermute | solution.py:145
  243.7 26.1 %collective-permute-start.32 = (bf16[144,1024]{1,0:T(8,128)(2,1)}, bf16[144,1024]{1,0:T(8,128)(2,1)}, u32[]{:S(2)}, u32[]{:S(2)}) collective-permute-start(bf16[144,1024]{1,0:T(8,128)(2,1)} %add_convert_fusion.19), channel_id=1, source_target_pairs={{0,16},{4,20},{8,24},{12,28},{16,0},{20,4},{24,8},{28,12},{1,17},{... | collective-permute-start | bytes 884744 | tf_op jit(solution)/shard_map/ppermute | solution.py:145
  248.2 26.3 %collective-permute-start.25 = (bf16[256,1152]{1,0:T(8,128)(2,1)}, bf16[256,1152]{1,0:T(8,128)(2,1)}, u32[]{:S(2)}, u32[]{:S(2)}) collective-permute-start(bf16[256,1152]{1,0:T(8,128)(2,1)} %constant_dynamic-slice_fusion.8), channel_id=1, source_target_pairs={{0,4},{4,0},{8,12},{12,8},{16,20},{20,16},{24,28},{28,24},{1,5},{5... | collective-permute-start | bytes 1769480 | tf_op jit(solution)/shard_map/ppermute | solution.py:145
  251.0 24.9 %collective-permute-start.24 = (bf16[256,1152]{1,0:T(8,128)(2,1)}, bf16[256,1152]{1,0:T(8,128)(2,1)}, u32[]{:S(2)}, u32[]{:S(2)}) collective-permute-start(bf16[256,1152]{1,0:T(8,128)(2,1)} %constant_dynamic-slice_fusion.9), channel_id=1, source_target_pairs={{0,8},{4,12},{8,0},{12,4},{16,24},{20,28},{24,16},{28,20},{1,9},{5... | collective-permute-start | bytes 1769480 | tf_op jit(solution)/shard_map/ppermute | solution.py:145
  258.0 6.2 %collective-permute-start.19 = (bf16[512,1024]{1,0:T(8,128)(2,1)}, bf16[512,1024]{1,0:T(8,128)(2,1)}, u32[]{:S(2)}, u32[]{:S(2)}) collective-permute-start(bf16[512,1024]{1,0:T(8,128)(2,1)} %constant_dynamic-slice_fusion.14), channel_id=1, source_target_pairs={{0,1},{1,0},{2,3},{3,2},{4,5},{5,4},{6,7},{7,6},{8,9},{9,8},{10,11... | collective-permute-start | bytes 3145736 | tf_op jit(solution)/shard_map/ppermute | solution.py:145
  261.6 49.8 %collective-permute-start.21 = (bf16[512,256]{1,0:T(8,128)(2,1)}, bf16[512,256]{1,0:T(8,128)(2,1)}, u32[]{:S(2)}, u32[]{:S(2)}) collective-permute-start(bf16[512,256]{1,0:T(8,128)(2,1)} %constant_dynamic-slice_fusion.12), channel_id=1, source_target_pairs={{0,8},{4,12},{8,0},{12,4},{16,24},{20,28},{24,16},{28,20},{1,9},{5... | collective-permute-start | bytes 786440 | tf_op jit(solution)/shard_map/ppermute | solution.py:145
  264.2 50.5 %collective-permute-start.37 = (bf16[512,1024]{1,0:T(8,128)(2,1)S(1)}, bf16[512,1024]{1,0:T(8,128)(2,1)S(1)}, u32[]{:S(2)}, u32[]{:S(2)}) collective-permute-start(bf16[512,1024]{1,0:T(8,128)(2,1)S(1)} %constant_dynamic-slice_fusion.1), channel_id=1, source_target_pairs={{0,1},{1,0},{2,3},{3,2},{4,5},{5,4},{6,7},{7,6},{8,9},{9,8},{10,11... | collective-permute-start | bytes 3145736 | tf_op jit(solution)/shard_map/ppermute | solution.py:145
  269.8 44.9 %collective-permute-start.38 = (bf16[512,1024]{1,0:T(8,128)(2,1)S(1)}, bf16[512,1024]{1,0:T(8,128)(2,1)S(1)}, u32[]{:S(2)}, u32[]{:S(2)}) collective-permute-start(bf16[512,1024]{1,0:T(8,128)(2,1)S(1)} %add_convert_fusion.7), channel_id=1, source_target_pairs={{0,2},{1,3},{2,0},{3,1},{4,6},{5,7},{6,4},{7,5},{8,10},{9,11},{10,... | collective-permute-start | bytes 3145736 | tf_op jit(solution)/shard_map/ppermute | solution.py:145
  274.5 14.2 %collective-permute-start.33 = (bf16[192,1024]{1,0:T(8,128)(2,1)S(1)}, bf16[192,1024]{1,0:T(8,128)(2,1)S(1)}, u32[]{:S(2)}, u32[]{:S(2)}) collective-permute-start(bf16[192,1024]{1,0:T(8,128)(2,1)S(1)} %pad_maximum_fusion.28), channel_id=1, source_target_pairs={{0,8},{4,12},{8,0},{12,4},{16,24},{20,28},{24,16},{28,20},{1,9},{5... | collective-permute-start | bytes 1179656 | tf_op jit(solution)/shard_map/ppermute | solution.py:145
  275.9 6.5 %collective-permute-start.34 = (bf16[96,1024]{1,0:T(8,128)(2,1)S(1)}, bf16[96,1024]{1,0:T(8,128)(2,1)S(1)}, u32[]{:S(2)}, u32[]{:S(2)}) collective-permute-start(bf16[96,1024]{1,0:T(8,128)(2,1)S(1)} %slice.163), channel_id=1, source_target_pairs={{0,4},{4,0},{8,12},{12,8},{16,20},{20,16},{24,28},{28,24},{1,5},{5... | collective-permute-start | bytes 589832 | tf_op jit(solution)/shard_map/ppermute | solution.py:145
  282.3 27.6 %collective-permute-start.26 = (bf16[256,1152]{1,0:T(8,128)(2,1)S(1)}, bf16[256,1152]{1,0:T(8,128)(2,1)S(1)}, u32[]{:S(2)}, u32[]{:S(2)}) collective-permute-start(bf16[256,1152]{1,0:T(8,128)(2,1)S(1)} %fusion.34), channel_id=1, source_target_pairs={{0,16},{4,20},{8,24},{12,28},{16,0},{20,4},{24,8},{28,12},{1,17},{... | collective-permute-start | bytes 1769480 | tf_op jit(solution)/shard_map/ppermute | solution.py:145
  288.7 22.7 %collective-permute-start.20 = (bf16[1536,256]{1,0:T(8,128)(2,1)S(1)}, bf16[1536,256]{1,0:T(8,128)(2,1)S(1)}, u32[]{:S(2)}, u32[]{:S(2)}) collective-permute-start(bf16[1536,256]{1,0:T(8,128)(2,1)S(1)} %constant_dynamic-slice_fusion.13), channel_id=1, source_target_pairs={{0,4},{4,0},{8,12},{12,8},{16,20},{20,16},{24,28},{28,24},{1,5},{5... | collective-permute-start | bytes 2359304 | tf_op jit(solution)/shard_map/ppermute | solution.py:145
  311.4 27.1 %collective-permute-start.43 = (bf16[256,1152]{1,0:T(8,128)(2,1)}, bf16[256,1152]{1,0:T(8,128)(2,1)}, u32[]{:S(2)}, u32[]{:S(2)}) collective-permute-start(bf16[256,1152]{1,0:T(8,128)(2,1)} %add_convert_fusion.13), channel_id=1, source_target_pairs={{0,16},{4,20},{8,24},{12,28},{16,0},{20,4},{24,8},{28,12},{1,17},{... | collective-permute-start | bytes 1769480 | tf_op jit(solution)/shard_map/ppermute | solution.py:145
  313.2 25.3 %collective-permute-start.36 = (bf16[256,256]{1,0:T(8,128)(2,1)}, bf16[256,256]{1,0:T(8,128)(2,1)S(1)}, u32[]{:S(2)}, u32[]{:S(2)}) collective-permute-start(bf16[256,256]{1,0:T(8,128)(2,1)} %constant_dynamic-slice_fusion.2), channel_id=1, source_target_pairs={{0,4},{4,0},{8,12},{12,8},{16,20},{20,16},{24,28},{28,24},{1,5},{5... | collective-permute-start | bytes 393224 | tf_op jit(solution)/shard_map/ppermute | solution.py:145
  319.1 24.0 %collective-permute-start.35 = (bf16[768,256]{1,0:T(8,128)(2,1)}, bf16[768,256]{1,0:T(8,128)(2,1)}, u32[]{:S(2)}, u32[]{:S(2)}) collective-permute-start(bf16[768,256]{1,0:T(8,128)(2,1)} %constant_dynamic-slice_fusion.3), channel_id=1, source_target_pairs={{0,8},{4,12},{8,0},{12,4},{16,24},{20,28},{24,16},{28,20},{1,9},{5... | collective-permute-start | bytes 1179656 | tf_op jit(solution)/shard_map/ppermute | solution.py:145
  347.2 14.2 %collective-permute-start.42 = (bf16[512,256]{1,0:T(8,128)(2,1)}, bf16[512,256]{1,0:T(8,128)(2,1)}, u32[]{:S(2)}, u32[]{:S(2)}) collective-permute-start(bf16[512,256]{1,0:T(8,128)(2,1)} %fusion.44), channel_id=1, source_target_pairs={{0,16},{4,20},{8,24},{12,28},{16,0},{20,4},{24,8},{28,12},{1,17},{... | collective-permute-start | bytes 786440 | tf_op jit(solution)/shard_map/ppermute | solution.py:145
  353.0 23.9 %collective-permute-start.57 = (bf16[384,1024]{1,0:T(8,128)(2,1)}, bf16[384,1024]{1,0:T(8,128)(2,1)S(1)}, u32[]{:S(2)}, u32[]{:S(2)}) collective-permute-start(bf16[384,1024]{1,0:T(8,128)(2,1)} %pad_maximum_fusion.25), channel_id=1, source_target_pairs={{0,4},{4,0},{8,12},{12,8},{16,20},{20,16},{24,28},{28,24},{1,5},{5... | collective-permute-start | bytes 2359304 | tf_op jit(solution)/shard_map/ppermute | solution.py:145
  353.5 24.0 %collective-permute-start.46 = (bf16[512,1024]{1,0:T(8,128)(2,1)}, bf16[512,1024]{1,0:T(8,128)(2,1)S(1)}, u32[]{:S(2)}, u32[]{:S(2)}) collective-permute-start(bf16[512,1024]{1,0:T(8,128)(2,1)} %add_convert_fusion.9), channel_id=1, source_target_pairs={{0,2},{1,3},{2,0},{3,1},{4,6},{5,7},{6,4},{7,5},{8,10},{9,11},{10,... | collective-permute-start | bytes 3145736 | tf_op jit(solution)/shard_map/ppermute | solution.py:145
  364.0 13.5 %collective-permute-start.45 = (bf16[512,1024]{1,0:T(8,128)(2,1)S(1)}, bf16[512,1024]{1,0:T(8,128)(2,1)S(1)}, u32[]{:S(2)}, u32[]{:S(2)}) collective-permute-start(bf16[512,1024]{1,0:T(8,128)(2,1)S(1)} %constant_dynamic-slice_fusion), channel_id=1, source_target_pairs={{0,1},{1,0},{2,3},{3,2},{4,5},{5,4},{6,7},{7,6},{8,9},{9,8},{10,11... | collective-permute-start | bytes 3145736 | tf_op jit(solution)/shard_map/ppermute | solution.py:145
  364.1 12.2 %collective-permute-start.58 = (bf16[192,1024]{1,0:T(8,128)(2,1)}, bf16[192,1024]{1,0:T(8,128)(2,1)S(1)}, u32[]{:S(2)}, u32[]{:S(2)}) collective-permute-start(bf16[192,1024]{1,0:T(8,128)(2,1)} %pad_maximum_fusion.29), channel_id=1, source_target_pairs={{0,8},{4,12},{8,0},{12,4},{16,24},{20,28},{24,16},{28,20},{1,9},{5... | collective-permute-start | bytes 1179656 | tf_op jit(solution)/shard_map/ppermute | solution.py:145
  368.3 25.8 %collective-permute-start.48 = (bf16[256,1152]{1,0:T(8,128)(2,1)S(1)}, bf16[256,1152]{1,0:T(8,128)(2,1)S(1)}, u32[]{:S(2)}, u32[]{:S(2)}) collective-permute-start(bf16[256,1152]{1,0:T(8,128)(2,1)S(1)} %copy-done.33), channel_id=1, source_target_pairs={{0,8},{4,12},{8,0},{12,4},{16,24},{20,28},{24,16},{28,20},{1,9},{5... | collective-permute-start | bytes 1769480 | tf_op jit(solution)/shard_map/ppermute | solution.py:145
  376.3 17.8 %collective-permute-start.49 = (bf16[256,1152]{1,0:T(8,128)(2,1)S(1)}, bf16[256,1152]{1,0:T(8,128)(2,1)S(1)}, u32[]{:S(2)}, u32[]{:S(2)}) collective-permute-start(bf16[256,1152]{1,0:T(8,128)(2,1)S(1)} %copy-done.34), channel_id=1, source_target_pairs={{0,4},{4,0},{8,12},{12,8},{16,20},{20,16},{24,28},{28,24},{1,5},{5... | collective-permute-start | bytes 1769480 | tf_op jit(solution)/shard_map/ppermute | solution.py:145
  377.2 24.1 %collective-permute-start.47 = (bf16[512,256]{1,0:T(8,128)(2,1)S(1)}, bf16[512,256]{1,0:T(8,128)(2,1)S(1)}, u32[]{:S(2)}, u32[]{:S(2)}) collective-permute-start(bf16[512,256]{1,0:T(8,128)(2,1)S(1)} %add_convert_fusion.20), channel_id=1, source_target_pairs={{0,16},{4,20},{8,24},{12,28},{16,0},{20,4},{24,8},{28,12},{1,17},{... | collective-permute-start | bytes 786440 | tf_op jit(solution)/shard_map/ppermute | solution.py:145
  396.8 40.1 %collective-permute-start.54 = (bf16[512,1152]{1,0:T(8,128)(2,1)}, bf16[512,1152]{1,0:T(8,128)(2,1)}, u32[]{:S(2)}, u32[]{:S(2)}) collective-permute-start(bf16[512,1152]{1,0:T(8,128)(2,1)} %pad_maximum_fusion.23), channel_id=1, source_target_pairs={{0,8},{4,12},{8,0},{12,4},{16,24},{20,28},{24,16},{28,20},{1,9},{5... | collective-permute-start | bytes 3538952 | tf_op jit(solution)/shard_map/ppermute | solution.py:145
  399.0 37.9 %collective-permute-start.53 = (bf16[512,1152]{1,0:T(8,128)(2,1)}, bf16[512,1152]{1,0:T(8,128)(2,1)}, u32[]{:S(2)}, u32[]{:S(2)}) collective-permute-start(bf16[512,1152]{1,0:T(8,128)(2,1)} %pad_maximum_fusion.22), channel_id=1, source_target_pairs={{0,4},{4,0},{8,12},{12,8},{16,20},{20,16},{24,28},{28,24},{1,5},{5... | collective-permute-start | bytes 3538952 | tf_op jit(solution)/shard_map/ppermute | solution.py:145
  401.4 32.1 %collective-permute-start.51 = (bf16[768,256]{1,0:T(8,128)(2,1)S(1)}, bf16[768,256]{1,0:T(8,128)(2,1)}, u32[]{:S(2)}, u32[]{:S(2)}) collective-permute-start(bf16[768,256]{1,0:T(8,128)(2,1)S(1)} %pad_maximum_fusion.27), channel_id=1, source_target_pairs={{0,8},{4,12},{8,0},{12,4},{16,24},{20,28},{24,16},{28,20},{1,9},{5... | collective-permute-start | bytes 1179656 | tf_op jit(solution)/shard_map/ppermute | solution.py:145
  404.3 24.7 %collective-permute-start.52 = (bf16[256,256]{1,0:T(8,128)(2,1)S(1)}, bf16[256,256]{1,0:T(8,128)(2,1)S(1)}, u32[]{:S(2)}, u32[]{:S(2)}) collective-permute-start(bf16[256,256]{1,0:T(8,128)(2,1)S(1)} %slice.164), channel_id=1, source_target_pairs={{0,4},{4,0},{8,12},{12,8},{16,20},{20,16},{24,28},{28,24},{1,5},{5... | collective-permute-start | bytes 393224 | tf_op jit(solution)/shard_map/ppermute | solution.py:145
  433.6 11.7 %collective-permute-start.56 = (bf16[512,256]{1,0:T(8,128)(2,1)S(1)}, bf16[512,256]{1,0:T(8,128)(2,1)S(1)}, u32[]{:S(2)}, u32[]{:S(2)}) collective-permute-start(bf16[512,256]{1,0:T(8,128)(2,1)S(1)} %pad_maximum_fusion.30), channel_id=1, source_target_pairs={{0,8},{4,12},{8,0},{12,4},{16,24},{20,28},{24,16},{28,20},{1,9},{5... | collective-permute-start | bytes 786440 | tf_op jit(solution)/shard_map/ppermute | solution.py:145
  436.2 17.7 %collective-permute-start.55 = (bf16[1536,256]{1,0:T(8,128)(2,1)S(1)}, bf16[1536,256]{1,0:T(8,128)(2,1)S(1)}, u32[]{:S(2)}, u32[]{:S(2)}) collective-permute-start(bf16[1536,256]{1,0:T(8,128)(2,1)S(1)} %pad_maximum_fusion.26), channel_id=1, source_target_pairs={{0,4},{4,0},{8,12},{12,8},{16,20},{20,16},{24,28},{28,24},{1,5},{5... | collective-permute-start | bytes 2359304 | tf_op jit(solution)/shard_map/ppermute | solution.py:145
  (110 other events, 725.7 us)
where the time goes:
time: 464 us; the launch traced here: 460 us
  waiting for transfers between devices  193 us (42%)
  matrix products  103 us (22%)
  other arithmetic  69.6 us (15%)
  starting transfers between devices  54.3 us (12%)
  local copies, waits for them, and re-layouts  37 us (8%)
    ppermute x59, waiting for transfers between devices, swap(): return lax.ppermute(values, axis, [(i, i ^ step) for i in range(count)])  193 us
    ppermute x59, starting transfers between devices, swap(): return lax.ppermute(values, axis, [(i, i ^ step) for i in range(count)])  54.3 us
    dot_general x10, matrix products, dot(): return jnp.dot(left, right, preferred_element_type=jnp.float32)  43.8 us
    dot_general x14, matrix products, dot_first(): lax.dot_general(left, right, (((0,), (0,)), ((), ())), preferred_element_...  30.5 us
    dot_general x10, matrix products, dot_last(): lax.dot_general(left, right, (((1,), (1,)), ((), ())), preferred_element_...  28.9 us
    unnamed x201, local copies, waits for them, and re-layouts  19.6 us
    dynamic_slice x20, local copies, waits for them, and re-layouts, part(): return lax.dynamic_slice_in_dim(values, index * size, size, axis=0)  13.5 us
    convert_element_type x14, other arithmetic, advance(): self.pieces = [(part(p, self.bit(step)).astype(jnp.float32) + got.astype(...  12.1 us
  transfers between devices with their start and end apart: 59, of which 24 were waited for; matrix products, arithmetic and copies ran while one was open for 35% of the time, Pallas kernels for 0%

commit v1 on v0

--- a/solution.py
+++ b/solution.py
@@ -356,10 +356,11 @@
     )
     back_sum = sum_far(back_far, core)
     back_crossed = swap(back_sum, "tensor", 2)
-    sum_down.advance(after=back_sum)
     gate_far, up_far = tied((gate_far, up_far), back_sum)
     grad_gate = (wgate_near + dot_first(two_far, gate_far)).astype(low)
     grad_up = (wup_near + dot_first(two_far, up_far)).astype(low)
+    sum_down.sent, grad_gate = lax.optimization_barrier((sum_down.sent, grad_gate))
+    sum_down.advance()
     sum_mlp = Sum(grad_gate, grad_up)
     sum_down.advance(after=grad_up)
     back_rows = reduce_near(tied(back_near, grad_gate), core, tied(back_crossed, grad_up))
@@ -394,22 +395,23 @@
     gains = small_sum(jnp.stack([gain_one, gain_two]), "tensor")
     out_crossed = swap(tied(out_sum, first_crossed), "tensor", 2)
     small = jnp.concatenate([gains.reshape(-1), (taps_near + taps_far).reshape(-1)])
-    done = (sum_mlp.pieces, sum_down.pieces)
+    last = sum_mlp
     step = 1
     for each in (
-        sum_mlp, sum_conv, sum_down, None, sum_conv, sum_mlp, None, sum_conv, sum_mlp, None,
-        sum_conv, sum_mlp, sum_conv, sum_conv,
+        sum_conv, sum_mlp, None, sum_down, sum_conv, sum_mlp, sum_conv, None, sum_conv, sum_mlp,
+        None, sum_conv, sum_mlp, sum_conv,
     ):
+        if each is None:
+            small, last.pieces = lax.optimization_barrier((small, last.pieces))
+            small = small + swap(small, "dp", step)
+            step *= 2
+            continue
         if each is sum_mlp and each.stage == 4:
-            result = resid + reduce_near(tied(out_near, done), core, out_crossed)
-            done = result
-        if each is None:
-            small = small + swap(tied(small, done), "dp", step)
-            step *= 2
-            done = small
-        else:
-            each.advance(after=done)
-            done = each.pieces
+            out_near, last.pieces = lax.optimization_barrier((out_near, last.pieces))
+            result = resid + reduce_near(out_near, core, out_crossed)
+        each.sent, last.pieces = lax.optimization_barrier((each.sent, last.pieces))
+        each.advance()
+        last = each
     grad_down = jnp.concatenate(sum_down.finish(), axis=0)
     grad_wgate, grad_wup = sum_mlp.finish()
     grad_blocks, grad_wout = sum_conv.finish()

time: 464 us -> 465 us (level)
  waiting for transfers between devices: 193 us -> 215 us
  other arithmetic: 69.6 us -> 59.1 us
  starting transfers between devices: 54.3 us -> 45.7 us
    ppermute x59, waiting for transfers between devices: 193 us -> 215 us  [swap(): return lax.ppermute(values, axis, [(i, i ^ step) for i in range(count)])]
    ppermute x59, starting transfers between devices: 54.3 us -> 45.7 us  [swap(): return lax.ppermute(values, axis, [(i, i ^ step) for i in range(count)])]
    convert_element_type x14, other arithmetic: 12.1 us -> 5.3 us  [advance(): self.pieces = [(part(p, self.bit(step)).astype(jnp.float32) + got.astype(...]
    unnamed x201 -> x183, local copies, waits for them, and re-layouts: 19.6 us -> 19.5 us
  transfers between devices with their start and end apart: 59 -> 59, of which waited for: 24 -> 24; matrix products, arithmetic and copies ran while one was open for 35% -> 31% of each run, Pallas kernels for 0% -> 0%
where the time goes in v1:
time: 465 us; the launch traced here: 460 us
  waiting for transfers between devices  215 us (46%)
  matrix products  103 us (22%)
  other arithmetic  59.1 us (13%)
  starting transfers between devices  45.7 us (10%)
  local copies, waits for them, and re-layouts  34.5 us (7%)
    ppermute x59, waiting for transfers between devices, swap(): return lax.ppermute(values, axis, [(i, i ^ step) for i in range(count)])  215 us
    ppermute x59, starting transfers between devices, swap(): return lax.ppermute(values, axis, [(i, i ^ step) for i in range(count)])  45.7 us
    dot_general x10, matrix products, dot(): return jnp.dot(left, right, preferred_element_type=jnp.float32)  43.7 us
    dot_general x14, matrix products, dot_first(): lax.dot_general(left, right, (((0,), (0,)), ((), ())), preferred_element_...  30.5 us
    dot_general x10, matrix products, dot_last(): lax.dot_general(left, right, (((1,), (1,)), ((), ())), preferred_element_...  28.8 us
    unnamed x183, local copies, waits for them, and re-layouts  19.5 us
    select_n x22, other arithmetic, in_order(): jnp.where(bit == 0, mine, other)  11 us
    dynamic_slice x20, local copies, waits for them, and re-layouts, part(): return lax.dynamic_slice_in_dim(values, index * size, size, axis=0)  10.2 us
  transfers between devices with their start and end apart: 59, of which 24 were waited for; matrix products, arithmetic and copies ran while one was open for 31% of the time, Pallas kernels for 0%

profile of v1, /device:TPU:0, one launch (start us, length us, event | category | flops | bytes accessed | tf_op | source)
XLA Modules:
  0.0 460.4 jit_solution(10659319526062096254)
XLA Ops:
  2.3 2.5 fusion.4
  5.3 2.6 collective-permute-start.2
  7.9 2.6 copy.21
  18.4 13.5 %collective-permute-done.2 = bf16[512,1024]{1,0:T(8,128)(2,1)} collective-permute-done((bf16[512,1024]{1,0:T(8,128)(2,1)}, bf16[512,1024]{1,0:T(8,128)(2,1)}, u32[]{:S(2)}, u32[]{:S(2)}) %collective-permute-start.2) | collective-permute-done | bytes 1048608 | tf_op jit(solution)/shard_map/ppermute | solution.py:145
  31.9 3.0 collective-permute-done.3
  50.1 23.4 %collective-permute-done.5 = bf16[512,1024]{1,0:T(8,128)(2,1)S(1)} collective-permute-done((bf16[512,1024]{1,0:T(8,128)(2,1)S(1)}, bf16[512,1024]{1,0:T(8,128)(2,1)S(1)}, u32[]{:S(2)}, u32[]{:S(2)}) %collective-permute-start.5) | collective-permute-done | bytes 1048608 | tf_op jit(solution)/shard_map/ppermute | solution.py:145
  76.6 2.9 fusion.20
  81.8 3.1 fusion.56
  85.0 6.7 %multiply_convert_fusion.5 = (bf16[1024,1152]{1,0:T(8,128)(2,1)}, bf16[1024,1152]{1,0:T(8,128)(2,1)S(1)}, bf16[1024,1152]{1,0:T(8,128)(2,1)}) fusion(f32[1024,1152]{1,0:T(8,128)S(1)} %fusion.56, f32[1024,1152]{1,0:T(8,128)S(1)} %fusion.20, bf16[1024,1152]{1,0:T(8,128)(2,1)S(1)} %copy-done, bf16[512,1024]{1,0:T(8,128)(2,1)S(1)} %get-tuple-element.220, ...), kind=kOutput, calls=%fused_computation.9 | convolution fusion | flops 2438987776 | bytes 20971520 | tf_op jit(solution)/shard_map/dot_general | solution.py:256
  91.7 2.9 fusion.64
  94.7 4.1 add_convert_fusion.4
  98.8 5.2 %collective-permute-done.8 = bf16[512,1024]{1,0:T(8,128)(2,1)S(1)} collective-permute-done((bf16[512,1024]{1,0:T(8,128)(2,1)S(1)}, bf16[512,1024]{1,0:T(8,128)(2,1)S(1)}, u32[]{:S(2)}, u32[]{:S(2)}) %collective-permute-start.8) | collective-permute-done | bytes 1048608 | tf_op jit(solution)/shard_map/ppermute | solution.py:145
  105.7 4.6 %fusion.53 = f32[1024,1152]{1,0:T(8,128)} fusion(bf16[1024,1152]{1,0:T(8,128)(2,1)S(1)} %copy-done.85, bf16[512,1024]{1,0:T(8,128)(2,1)S(1)} %get-tuple-element.220, bf16[512,1024]{1,0:T(8,128)(2,1)S(1)} %get-tuple-element.219), kind=kOutput, calls=%fused_computation.245 | convolution fusion | flops 2420113408 | bytes 9175040 | tf_op jit(solution)/shard_map/dot_general | solution.py:31
  110.3 4.6 fusion.54
  115.0 2.9 fusion.52
  117.9 17.5 %multiply_convert_fusion.2 = (bf16[1024,1152]{1,0:T(8,128)(2,1)S(1)}, f32[1024,1152]{1,0:T(8,128)}) fusion(f32[1024,1152]{1,0:T(8,128)S(1)} %fusion.52, bf16[1024,1152]{1,0:T(8,128)(2,1)S(1)} %copy-done, bf16[512,1024]{1,0:T(8,128)(2,1)S(1)} %get-tuple-element.216, bf16[512,1024]{1,0:T(8,128)(2,1)S(1)} %get-tuple-element.215), kind=kOutput, calls=%fused_computation.5 | convolution fusion | flops 2427191296 | bytes 16252928 | tf_op jit(solution)/shard_map/dot_general | solution.py:256
  135.4 3.1 convolution_convert_fusion
  138.8 2.7 fusion.19
  141.5 4.1 convolution_convert_fusion.1
  147.3 2.4 collective-permute-done.12
  149.8 4.0 add_convert_fusion.2
  154.0 5.9 %multiply_convert_fusion = (bf16[1024,1152]{1,0:T(8,128)(2,1)S(1)}, bf16[1024,1152]{1,0:T(8,128)(2,1)S(1)}) fusion(f32[1024,1152]{1,0:T(8,128)S(1)} %fusion.52, f32[1024,1152]{1,0:T(8,128)} %get-tuple-element.259, bf16[1024,1024]{1,0:T(8,128)(2,1)S(1)} %pad_maximum_fusion.7, bf16[1152,1024]{1,0:T(8,128)(2,1)S(1)} %copy-done.78), kind=kOutput, calls=%fused_computation.2 | convolution fusion | flops 2431254528 | bytes 18612224 | tf_op jit(solution)/shard_map/dot_general | solution.py:37
  159.9 2.9 fusion.65
  162.8 3.1 add_convert_fusion.3
  177.3 4.9 %add_convert_fusion.1 = bf16[1024,1152]{1,0:T(8,128)(2,1)S(1)} fusion(f32[1024,1152]{1,0:T(8,128)} %fusion.54, bf16[1024,1152]{1,0:T(8,128)(2,1)S(1)} %copy-done.83, bf16[512,1024]{1,0:T(8,128)(2,1)S(1)} %copy-done.58, bf16[512,1024]{1,0:T(8,128)(2,1)S(1)} %get-tuple-element.215), kind=kOutput, calls=%fused_computation.1 | convolution fusion | flops 2422472704 | bytes 11534336 | tf_op jit(solution)/shard_map/dot_general | solution.py:31
  182.9 9.8 %collective-permute-done.13 = bf16[384,1024]{1,0:T(8,128)(2,1)S(1)} collective-permute-done((bf16[384,1024]{1,0:T(8,128)(2,1)S(1)}, bf16[384,1024]{1,0:T(8,128)(2,1)S(1)}, u32[]{:S(2)}, u32[]{:S(2)}) %collective-permute-start.13) | collective-permute-done | bytes 786464 | tf_op jit(solution)/shard_map/ppermute | solution.py:145
  195.5 3.7 add_convert_fusion
  199.2 2.3 collective-permute-done.17
  206.2 19.5 %collective-permute-done.33 = bf16[96,1024]{1,0:T(8,128)(2,1)S(1)} collective-permute-done((bf16[96,1024]{1,0:T(8,128)(2,1)S(1)}, bf16[96,1024]{1,0:T(8,128)(2,1)S(1)}, u32[]{:S(2)}, u32[]{:S(2)}) %collective-permute-start.33) | collective-permute-done | bytes 196640 | tf_op jit(solution)/shard_map/ppermute | solution.py:145
  226.1 2.7 collective-permute-start.34
  232.8 3.1 convolution_convert_fusion.5
  235.9 4.1 collective-permute-done.25
  240.0 13.3 %collective-permute-done.19 = bf16[512,1024]{1,0:T(8,128)(2,1)S(1)} collective-permute-done((bf16[512,1024]{1,0:T(8,128)(2,1)S(1)}, bf16[512,1024]{1,0:T(8,128)(2,1)S(1)}, u32[]{:S(2)}, u32[]{:S(2)}) %collective-permute-start.19) | collective-permute-done | bytes 1048608 | tf_op jit(solution)/shard_map/ppermute | solution.py:145
  287.9 17.5 %collective-permute-done.37 = bf16[96,1024]{1,0:T(8,128)(2,1)S(1)} collective-permute-done((bf16[96,1024]{1,0:T(8,128)(2,1)S(1)}, bf16[96,1024]{1,0:T(8,128)(2,1)S(1)}, u32[]{:S(2)}, u32[]{:S(2)}) %collective-permute-start.37) | collective-permute-done | bytes 196640 | tf_op jit(solution)/shard_map/ppermute | solution.py:145
  309.3 23.8 %collective-permute-done.28 = bf16[256,1152]{1,0:T(8,128)(2,1)S(1)} collective-permute-done((bf16[256,1152]{1,0:T(8,128)(2,1)S(1)}, bf16[256,1152]{1,0:T(8,128)(2,1)S(1)}, u32[]{:S(2)}, u32[]{:S(2)}) %collective-permute-start.28) | collective-permute-done | bytes 589856 | tf_op jit(solution)/shard_map/ppermute | solution.py:145
  346.4 19.6 %collective-permute-done.30 = bf16[768,256]{1,0:T(8,128)(2,1)S(1)} collective-permute-done((bf16[768,256]{1,0:T(8,128)(2,1)S(1)}, bf16[768,256]{1,0:T(8,128)(2,1)S(1)}, u32[]{:S(2)}, u32[]{:S(2)}) %collective-permute-start.30) | collective-permute-done | bytes 393248 | tf_op jit(solution)/shard_map/ppermute | solution.py:145
  369.1 9.9 %collective-permute-done.44 = bf16[512,256]{1,0:T(8,128)(2,1)S(1)} collective-permute-done((bf16[512,256]{1,0:T(8,128)(2,1)S(1)}, bf16[512,256]{1,0:T(8,128)(2,1)S(1)}, u32[]{:S(2)}, u32[]{:S(2)}) %collective-permute-start.44) | collective-permute-done | bytes 262176 | tf_op jit(solution)/shard_map/ppermute | solution.py:145
  379.2 2.4 collective-permute-start.55
  381.5 2.7 maximum_convert_fusion
  384.2 6.1 %collective-permute-done.55 = f32[2816]{0:T(1024)S(1)} collective-permute-done((f32[2816]{0:T(1024)S(1)}, f32[2816]{0:T(1024)S(1)}, u32[]{:S(2)}, u32[]{:S(2)}) %collective-permute-start.55) | collective-permute-done | bytes 11296 | tf_op jit(solution)/shard_map/ppermute | solution.py:145
  390.3 3.5 collective-permute-done.45
  399.6 3.9 collective-permute-done.58
  411.6 3.6 add_add_fusion
  415.2 17.6 %collective-permute-done.52 = bf16[512,1152]{1,0:T(8,128)(2,1)} collective-permute-done((bf16[512,1152]{1,0:T(8,128)(2,1)S(1)}, bf16[512,1152]{1,0:T(8,128)(2,1)}, u32[]{:S(2)}, u32[]{:S(2)}) %collective-permute-start.52) | collective-permute-done | bytes 1179680 | tf_op jit(solution)/shard_map/ppermute | solution.py:145
  432.8 3.4 collective-permute-done.51
  441.1 8.6 %collective-permute-done.56 = bf16[1536,256]{1,0:T(8,128)(2,1)S(1)} collective-permute-done((bf16[1536,256]{1,0:T(8,128)(2,1)S(1)}, bf16[1536,256]{1,0:T(8,128)(2,1)S(1)}, u32[]{:S(2)}, u32[]{:S(2)}) %collective-permute-start.56) | collective-permute-done | bytes 786464 | tf_op jit(solution)/shard_map/ppermute | solution.py:145
  455.0 2.7 convert_element_type.414
  457.7 2.5 convert_element_type.415
  (413 shorter events, 136.4 us)
Async XLA Ops:
  5.3 26.6 %collective-permute-start.2 = (bf16[512,1024]{1,0:T(8,128)(2,1)}, bf16[512,1024]{1,0:T(8,128)(2,1)}, u32[]{:S(2)}, u32[]{:S(2)}) collective-permute-start(bf16[512,1024]{1,0:T(8,128)(2,1)} %fusion.4), channel_id=1, source_target_pairs={{0,2},{1,3},{2,0},{3,1},{4,6},{5,7},{6,4},{7,5},{8,10},{9,11},{10,... | collective-permute-start | bytes 3145736 | tf_op jit(solution)/shard_map/ppermute | solution.py:145
  48.2 25.3 %collective-permute-start.5 = (bf16[512,1024]{1,0:T(8,128)(2,1)S(1)}, bf16[512,1024]{1,0:T(8,128)(2,1)S(1)}, u32[]{:S(2)}, u32[]{:S(2)}) collective-permute-start(bf16[512,1024]{1,0:T(8,128)(2,1)S(1)} %add_convert_fusion.10), channel_id=1, source_target_pairs={{0,2},{1,3},{2,0},{3,1},{4,6},{5,7},{6,4},{7,5},{8,10},{9,11},{10,... | collective-permute-start | bytes 3145736 | tf_op jit(solution)/shard_map/ppermute | solution.py:145
  50.0 24.5 %collective-permute-start.7 = (bf16[512,1024]{1,0:T(8,128)(2,1)S(1)}, bf16[512,1024]{1,0:T(8,128)(2,1)S(1)}, u32[]{:S(2)}, u32[]{:S(2)}) collective-permute-start(bf16[512,1024]{1,0:T(8,128)(2,1)S(1)} %copy-done.25), channel_id=1, source_target_pairs={{0,1},{1,0},{2,3},{3,2},{4,5},{5,4},{6,7},{7,6},{8,9},{9,8},{10,11... | collective-permute-start | bytes 3145736 | tf_op jit(solution)/shard_map/ppermute | solution.py:145
  74.5 6.9 %collective-permute-start.6 = (bf16[512,1024]{1,0:T(8,128)(2,1)S(1)}, bf16[512,1024]{1,0:T(8,128)(2,1)S(1)}, u32[]{:S(2)}, u32[]{:S(2)}) collective-permute-start(bf16[512,1024]{1,0:T(8,128)(2,1)S(1)} %multiply_convert_fusion.6), channel_id=1, source_target_pairs={{0,1},{1,0},{2,3},{3,2},{4,5},{5,4},{6,7},{7,6},{8,9},{9,8},{10,11... | collective-permute-start | bytes 3145736 | tf_op jit(solution)/shard_map/ppermute | solution.py:145
  79.5 24.4 %collective-permute-start.8 = (bf16[512,1024]{1,0:T(8,128)(2,1)S(1)}, bf16[512,1024]{1,0:T(8,128)(2,1)S(1)}, u32[]{:S(2)}, u32[]{:S(2)}) collective-permute-start(bf16[512,1024]{1,0:T(8,128)(2,1)S(1)} %multiply_convert_fusion.6), channel_id=1, source_target_pairs={{0,2},{1,3},{2,0},{3,1},{4,6},{5,7},{6,4},{7,5},{8,10},{9,11},{10,... | collective-permute-start | bytes 3145736 | tf_op jit(solution)/shard_map/ppermute | solution.py:145
  104.0 10.9 %collective-permute-start.9 = (bf16[512,1024]{1,0:T(8,128)(2,1)S(1)}, bf16[512,1024]{1,0:T(8,128)(2,1)S(1)}, u32[]{:S(2)}, u32[]{:S(2)}) collective-permute-start(bf16[512,1024]{1,0:T(8,128)(2,1)S(1)} %collective-permute-done.8), channel_id=1, source_target_pairs={{0,1},{1,0},{2,3},{3,2},{4,5},{5,4},{6,7},{7,6},{8,9},{9,8},{10,11... | collective-permute-start | bytes 3145736 | tf_op jit(solution)/shard_map/ppermute | solution.py:145
  104.0 43.0 %collective-permute-start.10 = (bf16[512,1024]{1,0:T(8,128)(2,1)S(1)}, bf16[512,1024]{1,0:T(8,128)(2,1)S(1)}, u32[]{:S(2)}, u32[]{:S(2)}) collective-permute-start(bf16[512,1024]{1,0:T(8,128)(2,1)S(1)} %copy-done.25), channel_id=1, source_target_pairs={{0,2},{1,3},{2,0},{3,1},{4,6},{5,7},{6,4},{7,5},{8,10},{9,11},{10,... | collective-permute-start | bytes 3145736 | tf_op jit(solution)/shard_map/ppermute | solution.py:145
  138.6 7.0 %collective-permute-start.11 = (bf16[512,1024]{1,0:T(8,128)(2,1)S(1)}, bf16[512,1024]{1,0:T(8,128)(2,1)S(1)}, u32[]{:S(2)}, u32[]{:S(2)}) collective-permute-start(bf16[512,1024]{1,0:T(8,128)(2,1)S(1)} %constant_dynamic-slice_fusion.17), channel_id=1, source_target_pairs={{0,1},{1,0},{2,3},{3,2},{4,5},{5,4},{6,7},{7,6},{8,9},{9,8},{10,11... | collective-permute-start | bytes 3145736 | tf_op jit(solution)/shard_map/ppermute | solution.py:145
  171.6 11.3 %collective-permute-start.14 = (bf16[192,1024]{1,0:T(8,128)(2,1)S(1)}, bf16[192,1024]{1,0:T(8,128)(2,1)S(1)}, u32[]{:S(2)}, u32[]{:S(2)}) collective-permute-start(bf16[192,1024]{1,0:T(8,128)(2,1)S(1)} %constant_dynamic-slice_fusion.15), channel_id=1, source_target_pairs={{0,8},{4,12},{8,0},{12,4},{16,24},{20,28},{24,16},{28,20},{1,9},{5... | collective-permute-start | bytes 1179656 | tf_op jit(solution)/shard_map/ppermute | solution.py:145
  173.3 19.5 %collective-permute-start.13 = (bf16[384,1024]{1,0:T(8,128)(2,1)S(1)}, bf16[384,1024]{1,0:T(8,128)(2,1)S(1)}, u32[]{:S(2)}, u32[]{:S(2)}) collective-permute-start(bf16[384,1024]{1,0:T(8,128)(2,1)S(1)} %constant_dynamic-slice_fusion.16), channel_id=1, source_target_pairs={{0,4},{4,0},{8,12},{12,8},{16,20},{20,16},{24,28},{28,24},{1,5},{5... | collective-permute-start | bytes 2359304 | tf_op jit(solution)/shard_map/ppermute | solution.py:145
  176.7 24.8 %collective-permute-start.17 = (bf16[512,1024]{1,0:T(8,128)(2,1)S(1)}, bf16[512,1024]{1,0:T(8,128)(2,1)S(1)}, u32[]{:S(2)}, u32[]{:S(2)}) collective-permute-start(bf16[512,1024]{1,0:T(8,128)(2,1)S(1)} %add_convert_fusion.8), channel_id=1, source_target_pairs={{0,2},{1,3},{2,0},{3,1},{4,6},{5,7},{6,4},{7,5},{8,10},{9,11},{10,... | collective-permute-start | bytes 3145736 | tf_op jit(solution)/shard_map/ppermute | solution.py:145
  192.9 8.7 %collective-permute-start.16 = (bf16[512,1024]{1,0:T(8,128)(2,1)S(1)}, bf16[512,1024]{1,0:T(8,128)(2,1)S(1)}, u32[]{:S(2)}, u32[]{:S(2)}) collective-permute-start(bf16[512,1024]{1,0:T(8,128)(2,1)S(1)} %constant_dynamic-slice_fusion.13), channel_id=1, source_target_pairs={{0,1},{1,0},{2,3},{3,2},{4,5},{5,4},{6,7},{7,6},{8,9},{9,8},{10,11... | collective-permute-start | bytes 3145736 | tf_op jit(solution)/shard_map/ppermute | solution.py:145
  193.1 42.9 %collective-permute-start.24 = (bf16[512,1152]{1,0:T(8,128)(2,1)S(1)}, bf16[512,1152]{1,0:T(8,128)(2,1)S(1)}, u32[]{:S(2)}, u32[]{:S(2)}) collective-permute-start(bf16[512,1152]{1,0:T(8,128)(2,1)S(1)} %constant_dynamic-slice_fusion.9), channel_id=1, source_target_pairs={{0,4},{4,0},{8,12},{12,8},{16,20},{20,16},{24,28},{28,24},{1,5},{5... | collective-permute-start | bytes 3538952 | tf_op jit(solution)/shard_map/ppermute | solution.py:145
  195.0 30.7 %collective-permute-start.32 = (bf16[192,1024]{1,0:T(8,128)(2,1)S(1)}, bf16[192,1024]{1,0:T(8,128)(2,1)S(1)}, u32[]{:S(2)}, u32[]{:S(2)}) collective-permute-start(bf16[192,1024]{1,0:T(8,128)(2,1)S(1)} %constant_dynamic-slice_fusion.3), channel_id=1, source_target_pairs={{0,8},{4,12},{8,0},{12,4},{16,24},{20,28},{24,16},{28,20},{1,9},{5... | collective-permute-start | bytes 1179656 | tf_op jit(solution)/shard_map/ppermute | solution.py:145
  204.7 24.6 %collective-permute-start.18 = (bf16[512,1024]{1,0:T(8,128)(2,1)S(1)}, bf16[512,1024]{1,0:T(8,128)(2,1)S(1)}, u32[]{:S(2)}, u32[]{:S(2)}) collective-permute-start(bf16[512,1024]{1,0:T(8,128)(2,1)S(1)} %get-tuple-element.192), channel_id=1, source_target_pairs={{0,1},{1,0},{2,3},{3,2},{4,5},{5,4},{6,7},{7,6},{8,9},{9,8},{10,11... | collective-permute-start | bytes 3145736 | tf_op jit(solution)/shard_map/ppermute | solution.py:145
  204.9 20.8 %collective-permute-start.33 = (bf16[96,1024]{1,0:T(8,128)(2,1)S(1)}, bf16[96,1024]{1,0:T(8,128)(2,1)S(1)}, u32[]{:S(2)}, u32[]{:S(2)}) collective-permute-start(bf16[96,1024]{1,0:T(8,128)(2,1)S(1)} %constant_dynamic-slice_fusion.2), channel_id=1, source_target_pairs={{0,4},{4,0},{8,12},{12,8},{16,20},{20,16},{24,28},{28,24},{1,5},{5... | collective-permute-start | bytes 589832 | tf_op jit(solution)/shard_map/ppermute | solution.py:145
  205.5 34.5 %collective-permute-start.25 = (bf16[512,1152]{1,0:T(8,128)(2,1)S(1)}, bf16[512,1152]{1,0:T(8,128)(2,1)S(1)}, u32[]{:S(2)}, u32[]{:S(2)}) collective-permute-start(bf16[512,1152]{1,0:T(8,128)(2,1)S(1)} %constant_dynamic-slice_fusion.8), channel_id=1, source_target_pairs={{0,8},{4,12},{8,0},{12,4},{16,24},{20,28},{24,16},{28,20},{1,9},{5... | collective-permute-start | bytes 3538952 | tf_op jit(solution)/shard_map/ppermute | solution.py:145
  226.1 31.5 %collective-permute-start.34 = (bf16[144,1024]{1,0:T(8,128)(2,1)S(1)}, bf16[144,1024]{1,0:T(8,128)(2,1)S(1)}, u32[]{:S(2)}, u32[]{:S(2)}) collective-permute-start(bf16[144,1024]{1,0:T(8,128)(2,1)S(1)} %fusion.40), channel_id=1, source_target_pairs={{0,16},{4,20},{8,24},{12,28},{16,0},{20,4},{24,8},{28,12},{1,17},{... | collective-permute-start | bytes 884744 | tf_op jit(solution)/shard_map/ppermute | solution.py:145
  228.8 24.5 %collective-permute-start.19 = (bf16[512,1024]{1,0:T(8,128)(2,1)S(1)}, bf16[512,1024]{1,0:T(8,128)(2,1)S(1)}, u32[]{:S(2)}, u32[]{:S(2)}) collective-permute-start(bf16[512,1024]{1,0:T(8,128)(2,1)S(1)} %get-tuple-element.192), channel_id=1, source_target_pairs={{0,2},{1,3},{2,0},{3,1},{4,6},{5,7},{6,4},{7,5},{8,10},{9,11},{10,... | collective-permute-start | bytes 3145736 | tf_op jit(solution)/shard_map/ppermute | solution.py:145
  254.4 27.4 %collective-permute-start.27 = (bf16[256,1152]{1,0:T(8,128)(2,1)}, bf16[256,1152]{1,0:T(8,128)(2,1)}, u32[]{:S(2)}, u32[]{:S(2)}) collective-permute-start(bf16[256,1152]{1,0:T(8,128)(2,1)} %constant_dynamic-slice_fusion.6), channel_id=1, source_target_pairs={{0,4},{4,0},{8,12},{12,8},{16,20},{20,16},{24,28},{28,24},{1,5},{5... | collective-permute-start | bytes 1769480 | tf_op jit(solution)/shard_map/ppermute | solution.py:145
  257.2 24.7 %collective-permute-start.26 = (bf16[256,1152]{1,0:T(8,128)(2,1)}, bf16[256,1152]{1,0:T(8,128)(2,1)}, u32[]{:S(2)}, u32[]{:S(2)}) collective-permute-start(bf16[256,1152]{1,0:T(8,128)(2,1)} %constant_dynamic-slice_fusion.7), channel_id=1, source_target_pairs={{0,8},{4,12},{8,0},{12,4},{16,24},{20,28},{24,16},{28,20},{1,9},{5... | collective-permute-start | bytes 1769480 | tf_op jit(solution)/shard_map/ppermute | solution.py:145
  258.6 23.9 %collective-permute-start.35 = (bf16[144,1024]{1,0:T(8,128)(2,1)}, bf16[144,1024]{1,0:T(8,128)(2,1)}, u32[]{:S(2)}, u32[]{:S(2)}) collective-permute-start(bf16[144,1024]{1,0:T(8,128)(2,1)} %add_convert_fusion.19), channel_id=1, source_target_pairs={{0,16},{4,20},{8,24},{12,28},{16,0},{20,4},{24,8},{28,12},{1,17},{... | collective-permute-start | bytes 884744 | tf_op jit(solution)/shard_map/ppermute | solution.py:145
  265.6 7.0 %collective-permute-start.21 = (bf16[512,1024]{1,0:T(8,128)(2,1)}, bf16[512,1024]{1,0:T(8,128)(2,1)}, u32[]{:S(2)}, u32[]{:S(2)}) collective-permute-start(bf16[512,1024]{1,0:T(8,128)(2,1)} %constant_dynamic-slice_fusion.12), channel_id=1, source_target_pairs={{0,1},{1,0},{2,3},{3,2},{4,5},{5,4},{6,7},{7,6},{8,9},{9,8},{10,11... | collective-permute-start | bytes 3145736 | tf_op jit(solution)/shard_map/ppermute | solution.py:145
  269.1 37.8 %collective-permute-start.23 = (bf16[512,256]{1,0:T(8,128)(2,1)}, bf16[512,256]{1,0:T(8,128)(2,1)}, u32[]{:S(2)}, u32[]{:S(2)}) collective-permute-start(bf16[512,256]{1,0:T(8,128)(2,1)} %constant_dynamic-slice_fusion.10), channel_id=1, source_target_pairs={{0,8},{4,12},{8,0},{12,4},{16,24},{20,28},{24,16},{28,20},{1,9},{5... | collective-permute-start | bytes 786440 | tf_op jit(solution)/shard_map/ppermute | solution.py:145
  272.6 61.3 %collective-permute-start.40 = (bf16[512,1024]{1,0:T(8,128)(2,1)S(1)}, bf16[512,1024]{1,0:T(8,128)(2,1)S(1)}, u32[]{:S(2)}, u32[]{:S(2)}) collective-permute-start(bf16[512,1024]{1,0:T(8,128)(2,1)S(1)} %constant_dynamic-slice_fusion.1), channel_id=1, source_target_pairs={{0,1},{1,0},{2,3},{3,2},{4,5},{5,4},{6,7},{7,6},{8,9},{9,8},{10,11... | collective-permute-start | bytes 3145736 | tf_op jit(solution)/shard_map/ppermute | solution.py:145
  281.9 25.6 %collective-permute-start.22 = (bf16[1536,256]{1,0:T(8,128)(2,1)S(1)}, bf16[1536,256]{1,0:T(8,128)(2,1)S(1)}, u32[]{:S(2)}, u32[]{:S(2)}) collective-permute-start(bf16[1536,256]{1,0:T(8,128)(2,1)S(1)} %constant_dynamic-slice_fusion.11), channel_id=1, source_target_pairs={{0,4},{4,0},{8,12},{12,8},{16,20},{20,16},{24,28},{28,24},{1,5},{5... | collective-permute-start | bytes 2359304 | tf_op jit(solution)/shard_map/ppermute | solution.py:145
  283.6 22.3 %collective-permute-start.36 = (bf16[192,1024]{1,0:T(8,128)(2,1)S(1)}, bf16[192,1024]{1,0:T(8,128)(2,1)S(1)}, u32[]{:S(2)}, u32[]{:S(2)}) collective-permute-start(bf16[192,1024]{1,0:T(8,128)(2,1)S(1)} %pad_maximum_fusion.30), channel_id=1, source_target_pairs={{0,8},{4,12},{8,0},{12,4},{16,24},{20,28},{24,16},{28,20},{1,9},{5... | collective-permute-start | bytes 1179656 | tf_op jit(solution)/shard_map/ppermute | solution.py:145
  284.2 21.2 %collective-permute-start.37 = (bf16[96,1024]{1,0:T(8,128)(2,1)S(1)}, bf16[96,1024]{1,0:T(8,128)(2,1)S(1)}, u32[]{:S(2)}, u32[]{:S(2)}) collective-permute-start(bf16[96,1024]{1,0:T(8,128)(2,1)S(1)} %slice.163), channel_id=1, source_target_pairs={{0,4},{4,0},{8,12},{12,8},{16,20},{20,16},{24,28},{28,24},{1,5},{5... | collective-permute-start | bytes 589832 | tf_op jit(solution)/shard_map/ppermute | solution.py:145
  305.4 28.5 %collective-permute-start.41 = (bf16[512,1024]{1,0:T(8,128)(2,1)S(1)}, bf16[512,1024]{1,0:T(8,128)(2,1)S(1)}, u32[]{:S(2)}, u32[]{:S(2)}) collective-permute-start(bf16[512,1024]{1,0:T(8,128)(2,1)S(1)} %add_convert_fusion.7), channel_id=1, source_target_pairs={{0,2},{1,3},{2,0},{3,1},{4,6},{5,7},{6,4},{7,5},{8,10},{9,11},{10,... | collective-permute-start | bytes 3145736 | tf_op jit(solution)/shard_map/ppermute | solution.py:145
  305.9 27.2 %collective-permute-start.28 = (bf16[256,1152]{1,0:T(8,128)(2,1)S(1)}, bf16[256,1152]{1,0:T(8,128)(2,1)S(1)}, u32[]{:S(2)}, u32[]{:S(2)}) collective-permute-start(bf16[256,1152]{1,0:T(8,128)(2,1)S(1)} %fusion.33), channel_id=1, source_target_pairs={{0,16},{4,20},{8,24},{12,28},{16,0},{20,4},{24,8},{28,12},{1,17},{... | collective-permute-start | bytes 1769480 | tf_op jit(solution)/shard_map/ppermute | solution.py:145
  307.0 37.1 %collective-permute-start.39 = (bf16[192,1024]{1,0:T(8,128)(2,1)S(1)}, bf16[192,1024]{1,0:T(8,128)(2,1)S(1)}, u32[]{:S(2)}, u32[]{:S(2)}) collective-permute-start(bf16[192,1024]{1,0:T(8,128)(2,1)S(1)} %pad_maximum_fusion.31), channel_id=1, source_target_pairs={{0,8},{4,12},{8,0},{12,4},{16,24},{20,28},{24,16},{28,20},{1,9},{5... | collective-permute-start | bytes 1179656 | tf_op jit(solution)/shard_map/ppermute | solution.py:145
  307.5 38.1 %collective-permute-start.38 = (bf16[384,1024]{1,0:T(8,128)(2,1)S(1)}, bf16[384,1024]{1,0:T(8,128)(2,1)S(1)}, u32[]{:S(2)}, u32[]{:S(2)}) collective-permute-start(bf16[384,1024]{1,0:T(8,128)(2,1)S(1)} %pad_maximum_fusion.25), channel_id=1, source_target_pairs={{0,4},{4,0},{8,12},{12,8},{16,20},{20,16},{24,28},{28,24},{1,5},{5... | collective-permute-start | bytes 2359304 | tf_op jit(solution)/shard_map/ppermute | solution.py:145
  333.2 13.2 %collective-permute-start.31 = (bf16[256,256]{1,0:T(8,128)(2,1)S(1)}, bf16[256,256]{1,0:T(8,128)(2,1)S(1)}, u32[]{:S(2)}, u32[]{:S(2)}) collective-permute-start(bf16[256,256]{1,0:T(8,128)(2,1)S(1)} %constant_dynamic-slice_fusion.4), channel_id=1, source_target_pairs={{0,4},{4,0},{8,12},{12,8},{16,20},{20,16},{24,28},{28,24},{1,5},{5... | collective-permute-start | bytes 393224 | tf_op jit(solution)/shard_map/ppermute | solution.py:145
  335.1 31.7 %collective-permute-start.29 = (bf16[256,1152]{1,0:T(8,128)(2,1)S(1)}, bf16[256,1152]{1,0:T(8,128)(2,1)S(1)}, u32[]{:S(2)}, u32[]{:S(2)}) collective-permute-start(bf16[256,1152]{1,0:T(8,128)(2,1)S(1)} %add_convert_fusion.13), channel_id=1, source_target_pairs={{0,16},{4,20},{8,24},{12,28},{16,0},{20,4},{24,8},{28,12},{1,17},{... | collective-permute-start | bytes 1769480 | tf_op jit(solution)/shard_map/ppermute | solution.py:145
  343.7 22.3 %collective-permute-start.30 = (bf16[768,256]{1,0:T(8,128)(2,1)S(1)}, bf16[768,256]{1,0:T(8,128)(2,1)S(1)}, u32[]{:S(2)}, u32[]{:S(2)}) collective-permute-start(bf16[768,256]{1,0:T(8,128)(2,1)S(1)} %constant_dynamic-slice_fusion.5), channel_id=1, source_target_pairs={{0,8},{4,12},{8,0},{12,4},{16,24},{20,28},{24,16},{28,20},{1,9},{5... | collective-permute-start | bytes 1179656 | tf_op jit(solution)/shard_map/ppermute | solution.py:145
  344.1 66.0 %collective-permute-start.48 = (bf16[512,1024]{1,0:T(8,128)(2,1)}, bf16[512,1024]{1,0:T(8,128)(2,1)}, u32[]{:S(2)}, u32[]{:S(2)}) collective-permute-start(bf16[512,1024]{1,0:T(8,128)(2,1)} %add_convert_fusion.9), channel_id=1, source_target_pairs={{0,2},{1,3},{2,0},{3,1},{4,6},{5,7},{6,4},{7,5},{8,10},{9,11},{10,... | collective-permute-start | bytes 3145736 | tf_op jit(solution)/shard_map/ppermute | solution.py:145
  366.6 12.4 %collective-permute-start.44 = (bf16[512,256]{1,0:T(8,128)(2,1)S(1)}, bf16[512,256]{1,0:T(8,128)(2,1)S(1)}, u32[]{:S(2)}, u32[]{:S(2)}) collective-permute-start(bf16[512,256]{1,0:T(8,128)(2,1)S(1)} %fusion.42), channel_id=1, source_target_pairs={{0,16},{4,20},{8,24},{12,28},{16,0},{20,4},{24,8},{28,12},{1,17},{... | collective-permute-start | bytes 786440 | tf_op jit(solution)/shard_map/ppermute | solution.py:145
  366.9 28.4 %collective-permute-start.49 = (bf16[256,1152]{1,0:T(8,128)(2,1)S(1)}, bf16[256,1152]{1,0:T(8,128)(2,1)S(1)}, u32[]{:S(2)}, u32[]{:S(2)}) collective-permute-start(bf16[256,1152]{1,0:T(8,128)(2,1)S(1)} %get-tuple-element.130), channel_id=1, source_target_pairs={{0,8},{4,12},{8,0},{12,4},{16,24},{20,28},{24,16},{28,20},{1,9},{5... | collective-permute-start | bytes 1769480 | tf_op jit(solution)/shard_map/ppermute | solution.py:145
  369.1 26.1 %collective-permute-start.50 = (bf16[256,1152]{1,0:T(8,128)(2,1)S(1)}, bf16[256,1152]{1,0:T(8,128)(2,1)S(1)}, u32[]{:S(2)}, u32[]{:S(2)}) collective-permute-start(bf16[256,1152]{1,0:T(8,128)(2,1)S(1)} %get-tuple-element.134), channel_id=1, source_target_pairs={{0,4},{4,0},{8,12},{12,8},{16,20},{20,16},{24,28},{28,24},{1,5},{5... | collective-permute-start | bytes 1769480 | tf_op jit(solution)/shard_map/ppermute | solution.py:145
  379.1 14.7 %collective-permute-start.45 = (bf16[512,256]{1,0:T(8,128)(2,1)S(1)}, bf16[512,256]{1,0:T(8,128)(2,1)S(1)}, u32[]{:S(2)}, u32[]{:S(2)}) collective-permute-start(bf16[512,256]{1,0:T(8,128)(2,1)S(1)} %add_convert_fusion.20), channel_id=1, source_target_pairs={{0,16},{4,20},{8,24},{12,28},{16,0},{20,4},{24,8},{28,12},{1,17},{... | collective-permute-start | bytes 786440 | tf_op jit(solution)/shard_map/ppermute | solution.py:145
  379.2 11.1 %collective-permute-start.55 = (f32[2816]{0:T(1024)S(1)}, f32[2816]{0:T(1024)S(1)}, u32[]{:S(2)}, u32[]{:S(2)}) collective-permute-start(f32[2816]{0:T(1024)S(1)} %add.450), channel_id=1, source_target_pairs={{0,8},{4,12},{8,0},{12,4},{16,24},{20,28},{24,16},{28,20},{1,9},{5... | collective-permute-start | bytes 33800 | tf_op jit(solution)/shard_map/ppermute | solution.py:145
  395.2 12.5 %collective-permute-start.53 = (bf16[768,256]{1,0:T(8,128)(2,1)}, bf16[768,256]{1,0:T(8,128)(2,1)}, u32[]{:S(2)}, u32[]{:S(2)}) collective-permute-start(bf16[768,256]{1,0:T(8,128)(2,1)} %pad_maximum_fusion.29), channel_id=1, source_target_pairs={{0,8},{4,12},{8,0},{12,4},{16,24},{20,28},{24,16},{28,20},{1,9},{5... | collective-permute-start | bytes 1179656 | tf_op jit(solution)/shard_map/ppermute | solution.py:145
  395.2 11.8 %collective-permute-start.54 = (bf16[256,256]{1,0:T(8,128)(2,1)}, bf16[256,256]{1,0:T(8,128)(2,1)S(1)}, u32[]{:S(2)}, u32[]{:S(2)}) collective-permute-start(bf16[256,256]{1,0:T(8,128)(2,1)} %slice.164), channel_id=1, source_target_pairs={{0,4},{4,0},{8,12},{12,8},{16,20},{20,16},{24,28},{28,24},{1,5},{5... | collective-permute-start | bytes 393224 | tf_op jit(solution)/shard_map/ppermute | solution.py:145
  399.6 11.9 %collective-permute-start.47 = (bf16[512,1024]{1,0:T(8,128)(2,1)}, bf16[512,1024]{1,0:T(8,128)(2,1)}, u32[]{:S(2)}, u32[]{:S(2)}) collective-permute-start(bf16[512,1024]{1,0:T(8,128)(2,1)} %constant_dynamic-slice_fusion), channel_id=1, source_target_pairs={{0,1},{1,0},{2,3},{3,2},{4,5},{5,4},{6,7},{7,6},{8,9},{9,8},{10,11... | collective-permute-start | bytes 3145736 | tf_op jit(solution)/shard_map/ppermute | solution.py:145
  403.6 29.2 %collective-permute-start.52 = (bf16[512,1152]{1,0:T(8,128)(2,1)S(1)}, bf16[512,1152]{1,0:T(8,128)(2,1)}, u32[]{:S(2)}, u32[]{:S(2)}) collective-permute-start(bf16[512,1152]{1,0:T(8,128)(2,1)S(1)} %pad_maximum_fusion.24), channel_id=1, source_target_pairs={{0,8},{4,12},{8,0},{12,4},{16,24},{20,28},{24,16},{28,20},{1,9},{5... | collective-permute-start | bytes 3538952 | tf_op jit(solution)/shard_map/ppermute | solution.py:145
  407.0 29.2 %collective-permute-start.51 = (bf16[512,1152]{1,0:T(8,128)(2,1)}, bf16[512,1152]{1,0:T(8,128)(2,1)S(1)}, u32[]{:S(2)}, u32[]{:S(2)}) collective-permute-start(bf16[512,1152]{1,0:T(8,128)(2,1)} %pad_maximum_fusion.23), channel_id=1, source_target_pairs={{0,4},{4,0},{8,12},{12,8},{16,20},{20,16},{24,28},{28,24},{1,5},{5... | collective-permute-start | bytes 3538952 | tf_op jit(solution)/shard_map/ppermute | solution.py:145
  408.7 32.4 %collective-permute-start.57 = (bf16[512,256]{1,0:T(8,128)(2,1)S(1)}, bf16[512,256]{1,0:T(8,128)(2,1)S(1)}, u32[]{:S(2)}, u32[]{:S(2)}) collective-permute-start(bf16[512,256]{1,0:T(8,128)(2,1)S(1)} %pad_maximum_fusion.32), channel_id=1, source_target_pairs={{0,8},{4,12},{8,0},{12,4},{16,24},{20,28},{24,16},{28,20},{1,9},{5... | collective-permute-start | bytes 786440 | tf_op jit(solution)/shard_map/ppermute | solution.py:145
  410.1 39.7 %collective-permute-start.56 = (bf16[1536,256]{1,0:T(8,128)(2,1)S(1)}, bf16[1536,256]{1,0:T(8,128)(2,1)S(1)}, u32[]{:S(2)}, u32[]{:S(2)}) collective-permute-start(bf16[1536,256]{1,0:T(8,128)(2,1)S(1)} %pad_maximum_fusion.27), channel_id=1, source_target_pairs={{0,4},{4,0},{8,12},{12,8},{16,20},{20,16},{24,28},{28,24},{1,5},{5... | collective-permute-start | bytes 2359304 | tf_op jit(solution)/shard_map/ppermute | solution.py:145
  (101 other events, 624.5 us)
